TPU v7x, 512 devices: a whole 4x8x8 slice. The times are simulated.
512 devices in a mesh: freq: 16 (over z, y_lo), brick: 32 (over y_hi, x, core).
Axes of the slice: x: 4, y: 8 (y_hi: 4, y_lo: 2; y = y_hi * 2 + y_lo), z: 8, core: 2. Of those that a mesh axis runs over, the one named last changes fastest.
Arguments:
- panels: bfloat16 [16, 2, 1024, 24576], P('freq', None, 'brick'), may hold values from -6 to 6
- freq_weight: float32 [16], P('freq'), may hold values from 0.5 to 2
- surface_weight: float32 [4096], replicated, may hold values from 0.25 to 4
- picks: int32 [1024], replicated, may hold values from 0 to 4095, as said below
- neighbours: int32 [192, 13], P('brick'), may hold values from -1 to 191, as said below
Outputs:
- hessian: bfloat16 [192, 13, 128, 128], P('brick', None, 'freq')
Inputs may be any that keep to these rules, and one draw needn't show every extreme that they name: `picks`: strictly rising; the s-th entry lies in [s * 4, (s + 1) * 4). `neighbours`: bricks form a grid of 32 x 2 x 3 with id x * 2 * 3 + y * 3 + z. Row b lists, in an arbitrary order, the ids of the 13 bricks at offsets (1, dy, dz) for dy, dz in -1, 0, 1, (0, 1, dz) for dz in -1, 0, 1, and (0, 0, 1) from brick b, with -1 for an offset outside the grid.
All inputs are finite; a program needn't handle non-finite values.
Results may differ from a plain program's by a relative error of at most 0.022.
Values may be sent and summed in bfloat16 or wider, within the bound.
No kernel may reach another device: no remote copies, remote signals or barrier semaphores. Data moves between devices by JAX's collectives and lax.ppermute only.
A program may use at most 128 MiB of HBM per device.

v0:
```python
import math

import jax
import jax.numpy as jnp
from jax import lax
from jax.sharding import PartitionSpec as P


def passed_along(block, axis, distance):
    devices = range(lax.axis_size(axis))
    route = [(i - distance, i) for i in devices if i - distance in devices]
    return lax.ppermute(block, axis, route)


def shards(panels, freq_weight, surface_weight, picks, neighbours):
    freq_count, pair_parts, source_rows, cell_width = panels.shape
    brick_count = lax.axis_size("brick")
    local_bricks = neighbours.shape[0]
    cell_count = cell_width // (brick_count * local_bricks)
    slab_width = local_bricks * cell_count
    own_panels = lax.all_to_all(panels, "brick", split_axis=3, concat_axis=2, tiled=True)
    next_panels = passed_along(own_panels, "brick", -1)
    sources = own_panels.shape[2]
    total_freq = freq_count * lax.axis_size("freq")
    factor = 1.0 / math.sqrt(2 * sources * total_freq)
    weighting = freq_weight[:, None] * surface_weight[picks][None, :] * factor
    weighted = (own_panels * weighting[:, None, :, None]).astype(jnp.bfloat16)
    row_count = freq_count * pair_parts * sources
    weighted = weighted.reshape(row_count, slab_width)
    candidates = jnp.concatenate([own_panels, next_panels], axis=3).reshape(
        row_count, 2 * slab_width
    )
    products = lax.dot_general(
        weighted, candidates, (((0,), (0,)), ((), ())), preferred_element_type=jnp.float32
    )
    pair_blocks = products.reshape(
        local_bricks, cell_count, 2 * local_bricks, cell_count
    ).transpose(0, 2, 1, 3)
    present = neighbours >= 0
    relative = jnp.where(present, neighbours - lax.axis_index("brick") * local_bricks, 0)
    selector = (
        relative[:, :, None] == jnp.arange(2 * local_bricks, dtype=jnp.int32)[None, None, :]
    ) & present[:, :, None]
    selector = selector.astype(jnp.float32)
    rounded = jnp.einsum(
        "bkm,bmij->bkij", selector, pair_blocks, precision=lax.Precision.HIGHEST
    ).astype(jnp.bfloat16)
    summed = lax.psum(rounded, "freq").astype(jnp.float32)
    row_share = cell_count // lax.axis_size("freq")
    hessian = lax.dynamic_slice_in_dim(summed, lax.axis_index("freq") * row_share, row_share, 2)
    return hessian.astype(jnp.bfloat16)


def solution(mesh):
    in_specs = (P("freq", None, "brick", None), P("freq"), P(), P(), P("brick", None))
    out_specs = P("brick", None, "freq", None)
    return jax.shard_map(shards, mesh=mesh, in_specs=in_specs, out_specs=out_specs, check_vma=False)
```

profile of v0, /device:TPU:6, one launch (start us, length us, event | category | flops | bytes accessed | tf_op | source)
XLA Modules:
  0.0 441.8 jit_solution(9420162950280046580)
XLA Ops:
  6.5 0.0 copy-start
  6.5 0.0 all-reduce.2.cloned.1.call-start
  6.5 25.1 %copy.24 = bf16[1,2,32,24576]{2,1,0,3:T(2,128)(2,1)} copy(bf16[1,2,32,24576]{3,2,1,0:T(8,128)(2,1)} %param.5) | data formatting | bytes 6291456 | tf_op args[0]
  31.7 16.2 %reshape.41 = bf16[32,2,24576]{2,1,0:T(2,128)(2,1)S(1)} reshape(bf16[24576,1,2,32]{3,2,1,0:T(2,128)(2,1)} %bitcast.41) | data formatting | bytes 6291456
  47.9 83.3 %all_to_all.21 = bf16[32,2,24576]{2,1,0:T(2,128)(2,1)} all-to-all(bf16[32,2,24576]{2,1,0:T(2,128)(2,1)S(1)} %reshape.41), channel_id=1, replica_groups=mesh['freq'=16,'brick'=32] {'brick'}, dimensions={0} | all-to-all | bytes 6291456 | tf_op jit(solution)/shard_map/all_to_all | solution.py:21
  131.2 14.5 %reshape.42 = bf16[24576,1,2,32]{3,2,1,0:T(2,128)(2,1)} reshape(bf16[32,2,24576]{2,1,0:T(2,128)(2,1)} %all_to_all.21) | data formatting | bytes 6291456
  145.7 25.4 %copy.35 = bf16[1,2,32,32,768]{4,2,3,1,0:T(8,128)(2,1)S(1)} copy(bf16[1,2,32,32,768]{2,1,4,3,0:T(2,128)(2,1)} %bitcast.40) | data formatting | bytes 6291456 | tf_op jit(solution)/shard_map/all_to_all | solution.py:21
  171.2 1.9 collective-permute-start
  173.8 0.0 copy-done.4
  173.8 0.0 copy-done
  173.8 6.2 %gather_fusion = f32[1024]{0:T(1024)S(1)} fusion(f32[4096]{0:T(1024)S(1)} %copy-done, s32[1024]{0:T(1024)S(1)} %fusion.8), kind=kCustom, calls=%fused_computation | custom fusion | bytes 12288 | tf_op jit(solution)/shard_map/gather | solution.py:26
  180.0 2.3 fusion.2
  182.3 4.7 %copy.27 = bf16[768,2048]{1,0:T(8,128)(2,1)} copy(bf16[768,2048]{0,1:T(8,128)(2,1)} %fusion.2) | data formatting | bytes 6291456 | tf_op jit(solution)/shard_map/dot_general | solution.py:33
  187.0 20.9 %collective-permute-done = bf16[1,2,1024,768]{3,2,1,0:T(8,128)(2,1)} collective-permute-done((bf16[1,2,1024,768]{3,2,1,0:T(8,128)(2,1)S(1)}, bf16[1,2,1024,768]{3,2,1,0:T(8,128)(2,1)}, u32[]{:S(2)}, u32[]{:S(2)}) %collective-permute-start) | collective-permute-done | bytes 3145760 | tf_op jit(solution)/shard_map/ppermute | solution.py:12
  207.9 5.0 %maximum_bitcast_fusion = bf16[1536,2048]{0,1:T(8,128)(2,1)} fusion(bf16[2048,768]{1,0:T(8,128)(2,1)} %bitcast.14, bf16[2048,768]{1,0:T(8,128)(2,1)S(1)} %bitcast.43), kind=kLoop, calls=%fused_computation.1 | loop fusion | flops 12582912 | bytes 12582912 | tf_op jit(solution)/shard_map/dot_general | solution.py:33
  212.9 8.8 %copy.29 = bf16[1536,2048]{1,0:T(8,128)(2,1)} copy(bf16[1536,2048]{0,1:T(8,128)(2,1)} %maximum_bitcast_fusion) | data formatting | bytes 12582912 | tf_op jit(solution)/shard_map/dot_general | solution.py:33
  221.6 7.2 %convolution_bitcast_fusion = f32[6,12,128,128]{3,2,1,0:T(8,128)S(1)} fusion(bf16[6,128,2048,1]{2,1,3,0:T(8,128)(2,1)S(1)} %bitcast.45, bf16[12,128,2048,1]{2,1,0,3:T(8,128)(2,1)} %bitcast.44), kind=kOutput, calls=%fused_computation.7 | convolution fusion | flops 4831838208 | bytes 14155776 | tf_op jit(solution)/shard_map/dot_general | solution.py:33
  228.9 0.0 copy-start.1
  228.9 5.6 %fusion = bf16[6,13,128,128]{3,1,2,0:T(8,128)(2,1)S(1)} fusion(f32[6,12,128,128]{3,2,1,0:T(8,128)S(1)} %convolution_bitcast_fusion, s32[6,13]{1,0:T(8,128)S(1)} %subtract_select_fusion, pred[6,13]{1,0:T(8,128)(4,1)S(1)} %broadcast_compare_fusion), kind=kOutput, calls=%fused_computation.2 | convolution fusion | flops 184026960 | bytes 7274886 | tf_op jit(solution)/shard_map/bkm,bmij->bkij/dot_general | solution.py:45
  234.5 2.2 copy.42
  236.7 0.0 all-reduce.2.cloned.1.call-update
  236.7 196.6 %all-reduce.2.cloned.1.call-done = bf16[6,13,128,128]{3,2,1,0:T(8,128)(2,1)} async-done(((bf16[6,13,128,128]{3,2,1,0:T(8,128)(2,1)}), bf16[6,13,128,128]{3,2,1,0:T(8,128)(2,1)}) %all-reduce.2.cloned.1.call-update) | async-done | bytes 2555920 | tf_op jit(solution)/shard_map/psum | solution.py:48
  433.3 1.6 convert_convert_fusion
  434.9 0.0 copy-done.1
  (11 shorter events, 0.0 us)
Async XLA Ops:
  6.5 167.2 %copy-start = (f32[4096]{0:T(1024)S(1)}, f32[4096]{0:T(1024)}, u32[]{:S(2)}) copy-start(f32[4096]{0:T(1024)} %param.7) | copy-start | bytes 49156
  6.5 426.8 %all-reduce.2.cloned.1.call-start = ((), (), s32[]{:S(2)}) async-start(), calls=%async_computation.1 | async-start | bytes 5111808 | tf_op jit(solution)/shard_map/psum | solution.py:48
  145.7 28.0 %copy-start.4 = (s32[1024]{0:T(1024)S(1)}, s32[1024]{0:T(1024)}, u32[]{:S(2)}) copy-start(s32[1024]{0:T(1024)} %param.8) | copy-start | bytes 12292
  145.7 34.3 %copy-start.3 = (s32[6,13]{1,0:T(8,128)S(1)}, s32[6,13]{1,0:T(8,128)}, u32[]{:S(2)}) copy-start(s32[6,13]{1,0:T(8,128)} %param.9) | copy-start | bytes 940
  171.2 36.7 %collective-permute-start = (bf16[1,2,1024,768]{3,2,1,0:T(8,128)(2,1)S(1)}, bf16[1,2,1024,768]{3,2,1,0:T(8,128)(2,1)}, u32[]{:S(2)}, u32[]{:S(2)}) collective-permute-start(bf16[1,2,1024,768]{3,2,1,0:T(8,128)(2,1)S(1)} %bitcast.42), channel_id=1, source_target_pairs={{1,0},{2,1},{3,2},{4,3},{5,4},{6,5},{7,6},{8,7},{9,8},{10,9},{11,1... | collective-permute-start | bytes 9437192 | tf_op jit(solution)/shard_map/ppermute | solution.py:12
  212.9 8.8 %copy-start.2 = (bf16[768,2048]{1,0:T(8,128)(2,1)S(1)}, bf16[768,2048]{1,0:T(8,128)(2,1)}, u32[]{:S(2)}) copy-start(bf16[768,2048]{1,0:T(8,128)(2,1)} %copy.27) | copy-start | bytes 9437188
  228.9 206.1 %copy-start.1 = (f32[4096]{0:T(1024)S(1)}, f32[4096]{0:T(1024)}, u32[]{:S(2)}) copy-start(f32[4096]{0:T(1024)} %param.7) | copy-start | bytes 49156
Sparse Core Ops, SparseCore 0:
  236.8 196.4 all-reduce.1
where the time goes:
time: 445 us; the launch traced here: 442 us
  waiting for transfers between devices  217 us (49%)
  local copies, waits for them, and re-layouts  103 us (23%)
  blocking collectives  83.3 us (19%)
  between operations  14.2 us (3%)
  matrix products  12.8 us (3%)
  other arithmetic  8.87 us (2%)
    psum x1, waiting for transfers between devices, shards(): summed = lax.psum(rounded, 'freq').astype(jnp.float32)  197 us
    all_to_all x1, blocking collectives, shards(): lax.all_to_all(panels, 'brick', split_axis=3, concat_axis=2, tiled=True)  83.3 us
    unnamed x15, local copies, waits for them, and re-layouts  55.9 us
    all_to_all x1, local copies, waits for them, and re-layouts, shards(): lax.all_to_all(panels, 'brick', split_axis=3, concat_axis=2, tiled=True)  25.4 us
    ppermute x1, waiting for transfers between devices, passed_along(): return lax.ppermute(block, axis, route)  20.9 us
    dot_general x2, local copies, waits for them, and re-layouts, shards(): lax.dot_general(weighted, candidates, (((0,), (0,)), ((), ())), preferred...  13.5 us
  transfers between devices with their start and end apart: 2, of which 2 were waited for; matrix products, arithmetic and copies ran while one was open for 3% of the time, Pallas kernels for 0%

commit v1 on v0

v1 whole, which is shorter than its diff:
```python
import math

import jax
import jax.numpy as jnp
import numpy as np
from jax import lax
from jax.experimental import pallas as pl
from jax.experimental.pallas import tpu as pltpu
from jax.sharding import Mesh
from jax.sharding import PartitionSpec as P

CELLS = 128
BRICK_Y = 2
BRICK_Z = 3
SLAB = BRICK_Y * BRICK_Z
WIDTH = SLAB * CELLS
AXES = ("zh", "zl", "yl", "yh", "x", "core")
SIZES = (4, 2, 2, 4, 4, 2)
GATHER = ("yl", "zl", "x")
REDUCE = ("zh", "yh")

NEXT_PAIRS = [
    ((y * 3 + z, 6 + first), (y * 3 + z, 7 + first))
    for z, firsts in ((0, (0, 3)), (1, (0, 2, 4)), (2, (1, 4)))
    for y in range(BRICK_Y)
    for first in firsts
]
OWN_PAIRS = [
    ((0, 3), (0, 4)),
    ((1, 4), (1, 5)),
    ((2, 4), (2, 5)),
    ((0, 1), (1, 2)),
    ((1, 3), (3, 4)),
    ((4, 5), None),
]
PAIRS = NEXT_PAIRS + OWN_PAIRS
ROWS = 16 * len(PAIRS)
SHARES = 16


def block_table():
    table = np.full((SLAB, 2 * SLAB), 2 * len(PAIRS), np.int32)
    for at, pair in enumerate(PAIRS):
        for half, block in enumerate(pair):
            if block is not None:
                table[block] = 2 * at + half
    return table


def pack_kernel(scale_ref, own_ref, next_ref, out_ref):
    scale = scale_ref[...]
    width = own_ref.shape[1]
    out_ref[0, :, :width] = (own_ref[...].astype(jnp.float32) * scale).astype(jnp.bfloat16)
    out_ref[0, :, width:] = (next_ref[...].astype(jnp.float32) * scale).astype(jnp.bfloat16)


def pack(panels, scale):
    rows, cells = panels.shape
    pairs = cells // (2 * WIDTH)
    return pl.pallas_call(
        pack_kernel,
        grid=(pairs,),
        in_specs=[
            pl.BlockSpec((rows, 1), lambda c: (0, 0)),
            pl.BlockSpec((rows, 2 * WIDTH), lambda c: (0, c)),
            pl.BlockSpec((rows, WIDTH), lambda c: (0, (2 * c + 2) % (2 * pairs))),
        ],
        out_specs=pl.BlockSpec((1, rows, 3 * WIDTH), lambda c: (c, 0, 0)),
        out_shape=jax.ShapeDtypeStruct((pairs, rows, 3 * WIDTH), jnp.bfloat16),
        name="pack",
    )(scale, panels, panels)


def blocks_kernel(slab_ref, own_ref, next_ref, out_ref, turned):
    del slab_ref
    for brick in range(SLAB):
        turned[brick * CELLS : (brick + 1) * CELLS, :] = own_ref[:, brick * CELLS : (brick + 1) * CELLS].T

    def candidates(first, count):
        ref, first = (own_ref, first) if first < SLAB else (next_ref, first - SLAB)
        return ref[:, first * CELLS : (first + count) * CELLS]

    def product(bricks, first, count):
        left = jnp.concatenate([turned[b * CELLS : (b + 1) * CELLS, :] for b in bricks], axis=0)
        made = jnp.dot(left, candidates(first, count), preferred_element_type=jnp.float32)
        return {
            (b, first + n): made[m * CELLS : (m + 1) * CELLS, n * CELLS : (n + 1) * CELLS]
            for m, b in enumerate(bricks)
            for n in range(count)
        }

    def store(at, pair, made):
        parts = [
            made[b].reshape(SHARES, CELLS // SHARES, CELLS) if b is not None
            else jnp.zeros((SHARES, CELLS // SHARES, CELLS), jnp.float32)
            for b in pair
        ]
        out_ref[:, 16 * at : 16 * (at + 1), :] = jnp.concatenate(parts, axis=1).astype(jnp.bfloat16)

    for z, firsts in ((0, (0, 3)), (1, (0, 2, 4)), (2, (1, 4))):
        bricks = (z, 3 + z)
        for first in firsts:
            made = product(bricks, SLAB + first, 2)
            for at, pair in enumerate(PAIRS):
                if pair[0] in made:
                    store(at, pair, made)
    made = product((0, 1, 2), 3, 3)
    made.update({k: v for k, v in product((0, 1), 1, 2).items() if k in ((0, 1), (1, 2))})
    made.update({k: v for k, v in product((3, 4), 4, 2).items() if k in ((3, 4), (4, 5))})
    for at in range(len(NEXT_PAIRS), len(PAIRS)):
        store(at, PAIRS[at], made)


def blocks(gathered, slab):
    rows = gathered.shape[0]
    return pl.pallas_call(
        blocks_kernel,
        grid_spec=pltpu.PrefetchScalarGridSpec(
            num_scalar_prefetch=1,
            grid=(1,),
            in_specs=[
                pl.BlockSpec((rows, WIDTH), lambda i, s: (0, s[0])),
                pl.BlockSpec((rows, WIDTH), lambda i, s: (0, s[0] + 1)),
            ],
            out_specs=pl.BlockSpec((SHARES, ROWS, CELLS), lambda i, s: (0, 0, 0)),
            scratch_shapes=[pltpu.VMEM((WIDTH, rows), jnp.bfloat16)],
        ),
        out_shape=jax.ShapeDtypeStruct((SHARES, ROWS, CELLS), jnp.bfloat16),
        compiler_params=pltpu.CompilerParams(vmem_limit_bytes=40 * 1024 * 1024),
        cost_estimate=pl.CostEstimate(
            flops=2 * 48 * CELLS * CELLS * rows, bytes_accessed=2 * rows * 2 * WIDTH + 2 * SHARES * ROWS * CELLS, transcendentals=0
        ),
        name="blocks",
    )(slab, gathered, gathered)


def slots_kernel(index_ref, held_ref, out_ref):
    for b in range(out_ref.shape[0]):
        for k in range(out_ref.shape[1]):
            at = index_ref[b, k]
            out_ref[b, k] = held_ref[at]


def slots(held, index):
    share = held.shape[1]
    return pl.pallas_call(
        slots_kernel,
        in_specs=[pl.BlockSpec(memory_space=pltpu.SMEM), pl.BlockSpec(memory_space=pltpu.VMEM)],
        out_specs=pl.BlockSpec(memory_space=pltpu.VMEM),
        out_shape=jax.ShapeDtypeStruct((*index.shape, share, CELLS), jnp.bfloat16),
        name="slots",
    )(index, held)


def owner_route():
    route = []
    for source in range(math.prod(SIZES)):
        zh, zl, yl, yh, x, core = (int(v) for v in np.unravel_index(source, SIZES))
        target = np.ravel_multi_index((zh, yh // 2, yh % 2, yl * 2 + zl, x, core), SIZES)
        route.append((source, int(target)))
    return route


def row_scale(freq_weight, surface_weight, picks, total_rows):
    points = picks.shape[0]
    stride = surface_weight.shape[0] // points
    devices = lax.axis_size(("yh", "x", "core"))
    own = points // devices
    first = lax.axis_index(("yh", "x", "core")) * own
    own_picks = lax.dynamic_slice_in_dim(picks, first, own, 0)
    own_surface = lax.dynamic_slice_in_dim(surface_weight, first * stride, own * stride, 0).reshape(own, stride)
    offset = own_picks - (first + jnp.arange(own, dtype=jnp.int32)) * stride
    hit = offset[:, None] == jnp.arange(stride, dtype=jnp.int32)[None, :]
    picked = jnp.sum(jnp.where(hit, own_surface, 0.0), axis=1)
    return jnp.sqrt(freq_weight[0] * picked * (1.0 / math.sqrt(total_rows)))


def shards(panels, freq_weight, surface_weight, picks, neighbours):
    freq_count, parts, own_points, cells = panels.shape
    points = picks.shape[0]
    total_rows = parts * points * lax.axis_size(("zh", "zl", "yl"))
    scale = row_scale(freq_weight, surface_weight, picks, total_rows)
    scale = jnp.tile(scale, parts)[:, None]
    rows = parts * own_points
    packed = pack(panels.reshape(rows, cells), scale)
    gathered = lax.all_to_all(packed, GATHER, split_axis=0, concat_axis=0, tiled=True)
    gathered = gathered.reshape(-1, 3 * WIDTH)
    core = lax.axis_index("core")
    other = blocks(gathered, (1 - core).reshape(1))
    arrived = lax.ppermute(other, "core", [(0, 1), (1, 0)])
    own = blocks(gathered, core.reshape(1))
    partial = (own.astype(jnp.float32) + arrived.astype(jnp.float32)).astype(jnp.bfloat16)
    spread = lax.all_to_all(partial, REDUCE, split_axis=0, concat_axis=0, tiled=True)
    held = jnp.sum(spread.astype(jnp.float32), axis=0).astype(jnp.bfloat16)
    held = lax.ppermute(held, AXES, owner_route())
    slab = lax.axis_index(("yh", "x", "core"))
    relative = neighbours - slab * SLAB
    at = relative[:, :, None] == jnp.arange(2 * SLAB, dtype=jnp.int32)[None, None, :]
    at = at & (neighbours >= 0)[:, :, None]
    nothing = 2 * len(PAIRS)
    index = nothing + jnp.sum(jnp.where(at, jnp.asarray(block_table() - nothing)[:, None, :], 0), axis=2)
    share = CELLS // SHARES
    held = jnp.concatenate([held, jnp.zeros((share, CELLS), jnp.bfloat16)], axis=0)
    return slots(held.reshape(-1, share, CELLS), index.astype(jnp.int32))


def solution(mesh):
    fine = Mesh(mesh.devices.reshape(SIZES), AXES)
    freq, brick = ("zh", "zl", "yl"), ("yh", "x", "core")
    in_specs = (P(freq, None, brick, None), P(freq), P(), P(), P(brick, None))
    out_specs = P(brick, None, freq, None)
    return jax.shard_map(shards, mesh=fine, in_specs=in_specs, out_specs=out_specs, check_vma=False)
```

time: 445 us -> 179 us (0.40)
  the two profiles are of different devices: /device:TPU:6 before, /device:TPU:68 now
where the time goes in v1:
time: 179 us
  waiting for transfers between devices  115 us (64%)
  starting transfers between devices  36.6 us (20%)
  Pallas kernels  20.5 us (11%)
  other arithmetic  3.42 us (2%)
  local copies, waits for them, and re-layouts  2.22 us (1%)
    all_to_all x1, waiting for transfers between devices, shards(): lax.all_to_all(packed, GATHER, split_axis=0, concat_axis=0, tiled=True)  57.4 us
    all_to_all x1, waiting for transfers between devices, shards(): lax.all_to_all(partial, REDUCE, split_axis=0, concat_axis=0, tiled=True)  49.1 us
    all_to_all x1, starting transfers between devices, shards(): lax.all_to_all(partial, REDUCE, split_axis=0, concat_axis=0, tiled=True)  23.5 us
    pallas_call x1, Pallas kernels, pack(): pl.pallas_call(pack_kernel, grid=(pairs,), in_specs=[pl.BlockSpec((rows,...  11.4 us
    all_to_all x1, starting transfers between devices, shards(): lax.all_to_all(packed, GATHER, split_axis=0, concat_axis=0, tiled=True)  9.29 us
    ppermute x1, waiting for transfers between devices, shards(): held = lax.ppermute(held, AXES, owner_route())  8.61 us
    pallas_call x2, Pallas kernels, blocks(): pl.pallas_call(blocks_kernel, grid_spec=pltpu.PrefetchScalarGridSpec(num_...  7.45 us
  transfers between devices with their start and end apart: 4, of which 3 were waited for; matrix products, arithmetic and copies ran while one was open for 0% of the time, Pallas kernels for 2%

profile of v1, /device:TPU:68, one launch (start us, length us, event | category | flops | bytes accessed | tf_op | source)
XLA Modules:
  0.0 178.7 jit_solution(4865051759324659585)
XLA Ops:
  0.0 0.8 dynamic_slice.7
  0.8 0.1 reshape.28
  1.5 0.8 multiply_subtract_fusion
  2.3 0.2 select_reduce_fusion.1
  2.5 0.7 broadcast_in_dim_tile.4.scale_ref
  3.2 11.4 %pack.1 = bf16[16,64,2304]{2,1,0:T(8,128)(2,1)} custom-call(f32[64,1]{1,0:T(8,128)} %broadcast_in_dim_tile.4.scale_ref, bf16[64,24576]{1,0:T(8,128)(2,1)} %bitcast.8, bf16[64,24576]{1,0:T(8,128)(2,1)} %bitcast.9), custom_call_target="tpu_custom_call" | custom-call | tf_op jit(solution)/shard_map/pack/pallas_call | solution.py:60
  14.6 9.3 %all-to-all-start = ((bf16[16,64,2304]{2,1,0:T(8,128)(2,1)}), bf16[16,64,2304]{2,1,0:T(8,128)(2,1)}, u32[]{:S(2)}, u32[]{:S(2)}) async-start(bf16[16,64,2304]{2,1,0:T(8,128)(2,1)} %pack.1), calls=%async_computation | async-start | bytes 9437184 | tf_op jit(solution)/shard_map/all_to_all | solution.py:186
  23.9 57.4 %all-to-all-done = bf16[16,64,2304]{2,1,0:T(8,128)(2,1)} async-done(((bf16[16,64,2304]{2,1,0:T(8,128)(2,1)}), bf16[16,64,2304]{2,1,0:T(8,128)(2,1)}, u32[]{:S(2)}, u32[]{:S(2)}) %all-to-all-start) | async-done | bytes 4718624 | tf_op jit(solution)/shard_map/all_to_all | solution.py:186
  81.3 3.7 %blocks.3 = bf16[16,320,128]{2,1,0:T(8,128)(2,1)S(1)} custom-call(s32[1]{0:T(128)} %bitcast.4.slab_ref, bf16[1024,2304]{1,0:T(8,128)(2,1)} %bitcast.3.own_ref.next_ref, bf16[1024,2304]{1,0:T(8,128)(2,1)} %bitcast.3.own_ref.next_ref), custom_call_target="tpu_custom_call" | custom-call | flops 1610612736 | bytes 4456448 | tf_op jit(solution)/shard_map/blocks/pallas_call | solution.py:116
  85.0 1.9 %collective-permute-start = (bf16[16,320,128]{2,1,0:T(8,128)(2,1)S(1)}, bf16[16,320,128]{2,1,0:T(8,128)(2,1)S(1)}, u32[]{:S(2)}, u32[]{:S(2)}) collective-permute-start(bf16[16,320,128]{2,1,0:T(8,128)(2,1)S(1)} %blocks.3), channel_id=1, source_target_pairs={{0,1},{1,0},{2,3},{3,2},{4,5},{5,4},{6,7},{7,6},{8,9},{9,8},{10,11... | collective-permute-start | bytes 3932168 | tf_op jit(solution)/shard_map/ppermute | solution.py:190
  87.0 3.7 %blocks.2 = bf16[16,320,128]{2,1,0:T(8,128)(2,1)S(1)} custom-call(s32[1]{0:T(128)} %bitcast.slab_ref, bf16[1024,2304]{1,0:T(8,128)(2,1)} %bitcast.3.own_ref.next_ref, bf16[1024,2304]{1,0:T(8,128)(2,1)} %bitcast.3.own_ref.next_ref), custom_call_target="tpu_custom_call" | custom-call | flops 1610612736 | bytes 4456448 | tf_op jit(solution)/shard_map/blocks/pallas_call | solution.py:116
  90.7 0.0 collective-permute-done
  90.7 1.4 add_convert_fusion
  92.1 23.5 %all-to-all-start.1 = ((bf16[16,320,128]{2,1,0:T(8,128)(2,1)}), bf16[16,320,128]{2,1,0:T(8,128)(2,1)S(1)}, u32[]{:S(2)}, u32[]{:S(2)}) async-start(bf16[16,320,128]{2,1,0:T(8,128)(2,1)} %add_convert_fusion), calls=%async_computation.1 | async-start | bytes 2621440 | tf_op jit(solution)/shard_map/all_to_all | solution.py:193
  115.6 0.0 copy-done
  115.7 0.0 copy-done.1
  115.7 0.3 select_reduce_fusion
  115.9 49.1 %all-to-all-done.1 = bf16[16,320,128]{2,1,0:T(8,128)(2,1)S(1)} async-done(((bf16[16,320,128]{2,1,0:T(8,128)(2,1)}), bf16[16,320,128]{2,1,0:T(8,128)(2,1)S(1)}, u32[]{:S(2)}, u32[]{:S(2)}) %all-to-all-start.1) | async-done | bytes 1310752 | tf_op jit(solution)/shard_map/all_to_all | solution.py:193
  165.1 0.2 reduce_sum.32
  165.3 1.9 %collective-permute-start.1 = (bf16[320,128]{1,0:T(8,128)(2,1)S(1)}, bf16[320,128]{1,0:T(8,128)(2,1)S(1)}, u32[]{:S(2)}, u32[]{:S(2)}) collective-permute-start(bf16[320,128]{1,0:T(8,128)(2,1)S(1)} %reduce_sum.32), channel_id=1, source_target_pairs={{0,0},{1,1},{2,2},{3,3},{4,4},{5,5},{6,6},{7,7},{8,32},{9,33},{10,... | collective-permute-start | bytes 245768 | tf_op jit(solution)/shard_map/ppermute | solution.py:195
  167.2 0.6 broadcast_add_fusion.index_ref
  167.8 8.6 %collective-permute-done.1 = bf16[320,128]{1,0:T(8,128)(2,1)S(1)} collective-permute-done((bf16[320,128]{1,0:T(8,128)(2,1)S(1)}, bf16[320,128]{1,0:T(8,128)(2,1)S(1)}, u32[]{:S(2)}, u32[]{:S(2)}) %collective-permute-start.1) | collective-permute-done | bytes 81952 | tf_op jit(solution)/shard_map/ppermute | solution.py:195
  176.4 0.6 pad_bitcast_fusion.held_ref
  177.0 1.6 slots.1
  (6 shorter events, 0.0 us)
Async XLA Ops:
  14.6 66.7 %all-to-all-start = ((bf16[16,64,2304]{2,1,0:T(8,128)(2,1)}), bf16[16,64,2304]{2,1,0:T(8,128)(2,1)}, u32[]{:S(2)}, u32[]{:S(2)}) async-start(bf16[16,64,2304]{2,1,0:T(8,128)(2,1)} %pack.1), calls=%async_computation | async-start | bytes 9437184 | tf_op jit(solution)/shard_map/all_to_all | solution.py:186
  85.0 5.7 %collective-permute-start = (bf16[16,320,128]{2,1,0:T(8,128)(2,1)S(1)}, bf16[16,320,128]{2,1,0:T(8,128)(2,1)S(1)}, u32[]{:S(2)}, u32[]{:S(2)}) collective-permute-start(bf16[16,320,128]{2,1,0:T(8,128)(2,1)S(1)} %blocks.3), channel_id=1, source_target_pairs={{0,1},{1,0},{2,3},{3,2},{4,5},{5,4},{6,7},{7,6},{8,9},{9,8},{10,11... | collective-permute-start | bytes 3932168 | tf_op jit(solution)/shard_map/ppermute | solution.py:190
  92.1 23.5 %copy-start = (s32[6,13]{1,0:T(8,128)S(1)}, s32[6,13]{1,0:T(8,128)}, u32[]{:S(2)}) copy-start(s32[6,13]{1,0:T(8,128)} %param.10) | copy-start | bytes 940
  92.1 23.5 %copy-start.1 = (s32[6,12]{1,0:T(8,128)S(1)}, s32[6,12]{1,0:T(8,128)}, u32[]{:S(2)}) copy-start(s32[6,12]{1,0:T(8,128)} %constant.44.clone) | copy-start | bytes 868
  92.1 72.9 %all-to-all-start.1 = ((bf16[16,320,128]{2,1,0:T(8,128)(2,1)}), bf16[16,320,128]{2,1,0:T(8,128)(2,1)S(1)}, u32[]{:S(2)}, u32[]{:S(2)}) async-start(bf16[16,320,128]{2,1,0:T(8,128)(2,1)} %add_convert_fusion), calls=%async_computation.1 | async-start | bytes 2621440 | tf_op jit(solution)/shard_map/all_to_all | solution.py:193
  165.3 11.1 %collective-permute-start.1 = (bf16[320,128]{1,0:T(8,128)(2,1)S(1)}, bf16[320,128]{1,0:T(8,128)(2,1)S(1)}, u32[]{:S(2)}, u32[]{:S(2)}) collective-permute-start(bf16[320,128]{1,0:T(8,128)(2,1)S(1)} %reduce_sum.32), channel_id=1, source_target_pairs={{0,0},{1,1},{2,2},{3,3},{4,4},{5,5},{6,6},{7,7},{8,32},{9,33},{10,... | collective-permute-start | bytes 245768 | tf_op jit(solution)/shard_map/ppermute | solution.py:195

commit v2 on v1

--- a/solution.py
+++ b/solution.py
@@ -1,3 +1,4 @@
+import functools
 import math
 
 import jax
@@ -39,7 +40,7 @@
 
 
 def block_table():
-    table = np.full((SLAB, 2 * SLAB), 2 * len(PAIRS), np.int32)
+    table = np.full((SLAB, 2 * SLAB), -1, np.int32)
     for at, pair in enumerate(PAIRS):
         for half, block in enumerate(pair):
             if block is not None:
@@ -47,28 +48,50 @@
     return table
 
 
-def pack_kernel(scale_ref, own_ref, next_ref, out_ref):
-    scale = scale_ref[...]
-    width = own_ref.shape[1]
-    out_ref[0, :, :width] = (own_ref[...].astype(jnp.float32) * scale).astype(jnp.bfloat16)
-    out_ref[0, :, width:] = (next_ref[...].astype(jnp.float32) * scale).astype(jnp.bfloat16)
-
-
-def pack(panels, scale):
+def pack_kernel(freq_ref, surface_ref, picks_ref, own_ref, next_ref, out_ref, scale_ref, *, total_rows):
+    @pl.when(pl.program_id(0) == 0)
+    def _():
+        rows = scale_ref.shape[0]
+        own_points = rows // 2
+        first = lax.axis_index(("yh", "x", "core")) * own_points
+        row = lax.broadcasted_iota(jnp.int32, (own_points, CELLS), 0)
+        picked = jnp.zeros((own_points, CELLS), jnp.float32)
+        for point in range(own_points):
+            picked = jnp.where(row == point, surface_ref[picks_ref[first + point]], picked)
+        scale = jnp.sqrt(picked * (freq_ref[0] * (1.0 / math.sqrt(total_rows))))
+        scale_ref[:own_points] = scale
+        scale_ref[own_points:] = scale
+
+    scale = scale_ref[:, :1]
+    for pair in range(out_ref.shape[0]):
+        first = pair * 2 * WIDTH
+        if first + 3 * WIDTH <= own_ref.shape[1]:
+            out_ref[pair] = (own_ref[:, first : first + 3 * WIDTH].astype(jnp.float32) * scale).astype(jnp.bfloat16)
+        else:
+            out_ref[pair, :, : 2 * WIDTH] = (own_ref[:, first:].astype(jnp.float32) * scale).astype(jnp.bfloat16)
+            out_ref[pair, :, 2 * WIDTH :] = (next_ref[...].astype(jnp.float32) * scale).astype(jnp.bfloat16)
+
+
+def pack(panels, freq_weight, surface_weight, picks, total_rows):
     rows, cells = panels.shape
     pairs = cells // (2 * WIDTH)
+    step = 4
     return pl.pallas_call(
-        pack_kernel,
-        grid=(pairs,),
+        functools.partial(pack_kernel, total_rows=total_rows),
+        grid=(pairs // step,),
         in_specs=[
-            pl.BlockSpec((rows, 1), lambda c: (0, 0)),
-            pl.BlockSpec((rows, 2 * WIDTH), lambda c: (0, c)),
-            pl.BlockSpec((rows, WIDTH), lambda c: (0, (2 * c + 2) % (2 * pairs))),
+            pl.BlockSpec(memory_space=pltpu.SMEM),
+            pl.BlockSpec(memory_space=pltpu.SMEM),
+            pl.BlockSpec(memory_space=pltpu.SMEM),
+            pl.BlockSpec((rows, 2 * WIDTH * step), lambda c: (0, c)),
+            pl.BlockSpec((rows, WIDTH), lambda c: (0, (2 * step * (c + 1)) % (2 * pairs))),
         ],
-        out_specs=pl.BlockSpec((1, rows, 3 * WIDTH), lambda c: (c, 0, 0)),
+        out_specs=pl.BlockSpec((step, rows, 3 * WIDTH), lambda c: (c, 0, 0)),
         out_shape=jax.ShapeDtypeStruct((pairs, rows, 3 * WIDTH), jnp.bfloat16),
+        scratch_shapes=[pltpu.VMEM((rows, CELLS), jnp.float32)],
+        compiler_params=pltpu.CompilerParams(vmem_limit_bytes=24 * 1024 * 1024),
         name="pack",
-    )(scale, panels, panels)
+    )(freq_weight, surface_weight, picks, panels, panels)
 
 
 def blocks_kernel(slab_ref, own_ref, next_ref, out_ref, turned):
@@ -126,7 +149,7 @@
             scratch_shapes=[pltpu.VMEM((WIDTH, rows), jnp.bfloat16)],
         ),
         out_shape=jax.ShapeDtypeStruct((SHARES, ROWS, CELLS), jnp.bfloat16),
-        compiler_params=pltpu.CompilerParams(vmem_limit_bytes=40 * 1024 * 1024),
+        compiler_params=pltpu.CompilerParams(vmem_limit_bytes=24 * 1024 * 1024),
         cost_estimate=pl.CostEstimate(
             flops=2 * 48 * CELLS * CELLS * rows, bytes_accessed=2 * rows * 2 * WIDTH + 2 * SHARES * ROWS * CELLS, transcendentals=0
         ),
@@ -138,7 +161,8 @@
     for b in range(out_ref.shape[0]):
         for k in range(out_ref.shape[1]):
             at = index_ref[b, k]
-            out_ref[b, k] = held_ref[at]
+            block = held_ref[jnp.maximum(at, 0)]
+            out_ref[b, k] = jnp.where(at >= 0, block, jnp.zeros_like(block))
 
 
 def slots(held, index):
@@ -148,6 +172,7 @@
         in_specs=[pl.BlockSpec(memory_space=pltpu.SMEM), pl.BlockSpec(memory_space=pltpu.VMEM)],
         out_specs=pl.BlockSpec(memory_space=pltpu.VMEM),
         out_shape=jax.ShapeDtypeStruct((*index.shape, share, CELLS), jnp.bfloat16),
+        compiler_params=pltpu.CompilerParams(vmem_limit_bytes=16 * 1024 * 1024),
         name="slots",
     )(index, held)
 
@@ -161,28 +186,12 @@
     return route
 
 
-def row_scale(freq_weight, surface_weight, picks, total_rows):
-    points = picks.shape[0]
-    stride = surface_weight.shape[0] // points
-    devices = lax.axis_size(("yh", "x", "core"))
-    own = points // devices
-    first = lax.axis_index(("yh", "x", "core")) * own
-    own_picks = lax.dynamic_slice_in_dim(picks, first, own, 0)
-    own_surface = lax.dynamic_slice_in_dim(surface_weight, first * stride, own * stride, 0).reshape(own, stride)
-    offset = own_picks - (first + jnp.arange(own, dtype=jnp.int32)) * stride
-    hit = offset[:, None] == jnp.arange(stride, dtype=jnp.int32)[None, :]
-    picked = jnp.sum(jnp.where(hit, own_surface, 0.0), axis=1)
-    return jnp.sqrt(freq_weight[0] * picked * (1.0 / math.sqrt(total_rows)))
-
-
 def shards(panels, freq_weight, surface_weight, picks, neighbours):
     freq_count, parts, own_points, cells = panels.shape
     points = picks.shape[0]
     total_rows = parts * points * lax.axis_size(("zh", "zl", "yl"))
-    scale = row_scale(freq_weight, surface_weight, picks, total_rows)
-    scale = jnp.tile(scale, parts)[:, None]
     rows = parts * own_points
-    packed = pack(panels.reshape(rows, cells), scale)
+    packed = pack(panels.reshape(rows, cells), freq_weight, surface_weight, picks, total_rows)
     gathered = lax.all_to_all(packed, GATHER, split_axis=0, concat_axis=0, tiled=True)
     gathered = gathered.reshape(-1, 3 * WIDTH)
     core = lax.axis_index("core")
@@ -197,10 +206,8 @@
     relative = neighbours - slab * SLAB
     at = relative[:, :, None] == jnp.arange(2 * SLAB, dtype=jnp.int32)[None, None, :]
     at = at & (neighbours >= 0)[:, :, None]
-    nothing = 2 * len(PAIRS)
-    index = nothing + jnp.sum(jnp.where(at, jnp.asarray(block_table() - nothing)[:, None, :], 0), axis=2)
+    index = jnp.sum(jnp.where(at, jnp.asarray(block_table() + 1)[:, None, :], 0), axis=2) - 1
     share = CELLS // SHARES
-    held = jnp.concatenate([held, jnp.zeros((share, CELLS), jnp.bfloat16)], axis=0)
     return slots(held.reshape(-1, share, CELLS), index.astype(jnp.int32))
 
 

time: 179 us -> 172 us (0.961)
  Pallas kernels: 20.5 us -> 11.2 us
  local copies, waits for them, and re-layouts: 2.22 us -> 5.46 us
    pallas_call x1, Pallas kernels: 11.4 us -> 2.33 us  [pack(): pl.pallas_call(functools.partial(pack_kernel, total_rows=total_rows), gri...]
    unnamed x4 -> x12, local copies, waits for them, and re-layouts: 0.01 us -> 5.46 us
where the time goes in v2:
time: 172 us; the launch traced here: 171 us
  waiting for transfers between devices  115 us (67%)
  starting transfers between devices  36.6 us (21%)
  Pallas kernels  11.2 us (7%)
  local copies, waits for them, and re-layouts  5.46 us (3%)
  other arithmetic  1.88 us (1%)
    all_to_all x1, waiting for transfers between devices, shards(): lax.all_to_all(packed, GATHER, split_axis=0, concat_axis=0, tiled=True)  57.4 us
    all_to_all x1, waiting for transfers between devices, shards(): lax.all_to_all(partial, REDUCE, split_axis=0, concat_axis=0, tiled=True)  48.6 us
    all_to_all x1, starting transfers between devices, shards(): lax.all_to_all(partial, REDUCE, split_axis=0, concat_axis=0, tiled=True)  23.5 us
    all_to_all x1, starting transfers between devices, shards(): lax.all_to_all(packed, GATHER, split_axis=0, concat_axis=0, tiled=True)  9.29 us
    ppermute x1, waiting for transfers between devices, shards(): held = lax.ppermute(held, AXES, owner_route())  9.2 us
    pallas_call x2, Pallas kernels, blocks(): pl.pallas_call(blocks_kernel, grid_spec=pltpu.PrefetchScalarGridSpec(num_...  7.46 us
    unnamed x12, local copies, waits for them, and re-layouts  5.46 us
  transfers between devices with their start and end apart: 4, of which 3 were waited for; matrix products, arithmetic and copies ran while one was open for 0% of the time, Pallas kernels for 2%

profile of v2, /device:TPU:68, one launch (start us, length us, event | category | flops | bytes accessed | tf_op | source)
XLA Modules:
  0.0 171.1 jit_solution(7199772223415343596)
XLA Ops:
  0.7 0.0 copy-start.1
  0.7 1.9 %copy-done.1 = bf16[1,2,32,24576]{3,2,1,0:T(8,128)(2,1)S(1)} copy-done((bf16[1,2,32,24576]{3,2,1,0:T(8,128)(2,1)S(1)}, bf16[1,2,32,24576]{3,2,1,0:T(8,128)(2,1)}, u32[]{:S(2)}) %copy-start.1) | copy-done | bytes 3145752
  2.5 0.0 copy-start.2
  2.5 0.7 copy-done.2
  3.3 0.7 copy-done.3
  3.9 2.3 %pack.1 = bf16[16,64,2304]{2,1,0:T(8,128)(2,1)S(1)} custom-call(f32[1]{0:T(128)S(6)} %copy.7.freq_ref, f32[4096]{0:T(1024)S(1)} %copy-done.2, s32[1024]{0:T(1024)S(1)} %copy-done.3, bf16[64,24576]{1,0:T(8,128)(2,1)S(1)} %bitcast.5, bf16[64,24576]{1,0:T(8,128)(2,1)S(1)} %bitcast.6), custom_call_target="tpu_custom_call" | custom-call | tf_op jit(solution)/shard_map/pack/pallas_call | solution.py:79
  6.3 0.0 copy-start
  6.3 2.2 %copy-done = bf16[16,64,2304]{2,1,0:T(8,128)(2,1)} copy-done((bf16[16,64,2304]{2,1,0:T(8,128)(2,1)}, bf16[16,64,2304]{2,1,0:T(8,128)(2,1)S(1)}, u32[]{:S(2)}) %copy-start) | copy-done | bytes 4718616
  8.5 9.3 %all-to-all-start = ((bf16[16,64,2304]{2,1,0:T(8,128)(2,1)}), bf16[16,64,2304]{2,1,0:T(8,128)(2,1)}, u32[]{:S(2)}, u32[]{:S(2)}) async-start(bf16[16,64,2304]{2,1,0:T(8,128)(2,1)} %copy-done), calls=%async_computation | async-start | bytes 9437184 | tf_op jit(solution)/shard_map/all_to_all | solution.py:195
  17.8 57.4 %all-to-all-done = bf16[16,64,2304]{2,1,0:T(8,128)(2,1)} async-done(((bf16[16,64,2304]{2,1,0:T(8,128)(2,1)}), bf16[16,64,2304]{2,1,0:T(8,128)(2,1)}, u32[]{:S(2)}, u32[]{:S(2)}) %all-to-all-start) | async-done | bytes 4718624 | tf_op jit(solution)/shard_map/all_to_all | solution.py:195
  75.1 3.7 %blocks.3 = bf16[16,320,128]{2,1,0:T(8,128)(2,1)S(1)} custom-call(s32[1]{0:T(128)} %bitcast.3.slab_ref, bf16[1024,2304]{1,0:T(8,128)(2,1)} %bitcast.2.own_ref.next_ref, bf16[1024,2304]{1,0:T(8,128)(2,1)} %bitcast.2.own_ref.next_ref), custom_call_target="tpu_custom_call" | custom-call | flops 1610612736 | bytes 4456448 | tf_op jit(solution)/shard_map/blocks/pallas_call | solution.py:139
  78.9 1.9 %collective-permute-start = (bf16[16,320,128]{2,1,0:T(8,128)(2,1)S(1)}, bf16[16,320,128]{2,1,0:T(8,128)(2,1)S(1)}, u32[]{:S(2)}, u32[]{:S(2)}) collective-permute-start(bf16[16,320,128]{2,1,0:T(8,128)(2,1)S(1)} %blocks.3), channel_id=1, source_target_pairs={{0,1},{1,0},{2,3},{3,2},{4,5},{5,4},{6,7},{7,6},{8,9},{9,8},{10,11... | collective-permute-start | bytes 3932168 | tf_op jit(solution)/shard_map/ppermute | solution.py:199
  80.8 3.7 %blocks.2 = bf16[16,320,128]{2,1,0:T(8,128)(2,1)S(1)} custom-call(s32[1]{0:T(128)} %bitcast.slab_ref, bf16[1024,2304]{1,0:T(8,128)(2,1)} %bitcast.2.own_ref.next_ref, bf16[1024,2304]{1,0:T(8,128)(2,1)} %bitcast.2.own_ref.next_ref), custom_call_target="tpu_custom_call" | custom-call | flops 1610612736 | bytes 4456448 | tf_op jit(solution)/shard_map/blocks/pallas_call | solution.py:139
  84.5 0.0 collective-permute-done
  84.6 1.4 add_convert_fusion
  86.0 23.5 %all-to-all-start.1 = ((bf16[16,320,128]{2,1,0:T(8,128)(2,1)}), bf16[16,320,128]{2,1,0:T(8,128)(2,1)S(1)}, u32[]{:S(2)}, u32[]{:S(2)}) async-start(bf16[16,320,128]{2,1,0:T(8,128)(2,1)} %add_convert_fusion), calls=%async_computation.1 | async-start | bytes 2621440 | tf_op jit(solution)/shard_map/all_to_all | solution.py:202
  109.5 0.0 copy-done.4
  109.5 0.0 copy-done.5
  109.5 0.3 select_reduce_fusion
  109.8 48.6 %all-to-all-done.1 = bf16[16,320,128]{2,1,0:T(8,128)(2,1)S(1)} async-done(((bf16[16,320,128]{2,1,0:T(8,128)(2,1)}), bf16[16,320,128]{2,1,0:T(8,128)(2,1)S(1)}, u32[]{:S(2)}, u32[]{:S(2)}) %all-to-all-start.1) | async-done | bytes 1310752 | tf_op jit(solution)/shard_map/all_to_all | solution.py:202
  158.4 0.2 reduce_sum.22
  158.5 1.9 %collective-permute-start.1 = (bf16[320,128]{1,0:T(8,128)(2,1)S(1)}, bf16[320,128]{1,0:T(8,128)(2,1)S(1)}, u32[]{:S(2)}, u32[]{:S(2)}) collective-permute-start(bf16[320,128]{1,0:T(8,128)(2,1)S(1)} %reduce_sum.22), channel_id=1, source_target_pairs={{0,0},{1,1},{2,2},{3,3},{4,4},{5,5},{6,6},{7,7},{8,32},{9,33},{10,... | collective-permute-start | bytes 245768 | tf_op jit(solution)/shard_map/ppermute | solution.py:204
  160.5 9.2 %collective-permute-done.1 = bf16[320,128]{1,0:T(8,128)(2,1)S(1)} collective-permute-done((bf16[320,128]{1,0:T(8,128)(2,1)S(1)}, bf16[320,128]{1,0:T(8,128)(2,1)S(1)}, u32[]{:S(2)}, u32[]{:S(2)}) %collective-permute-start.1) | collective-permute-done | bytes 81952 | tf_op jit(solution)/shard_map/ppermute | solution.py:204
  169.7 1.4 slots.1
  (6 shorter events, 0.0 us)
Async XLA Ops:
  0.7 1.9 %copy-start.1 = (bf16[1,2,32,24576]{3,2,1,0:T(8,128)(2,1)S(1)}, bf16[1,2,32,24576]{3,2,1,0:T(8,128)(2,1)}, u32[]{:S(2)}) copy-start(bf16[1,2,32,24576]{3,2,1,0:T(8,128)(2,1)} %param.6) | copy-start | bytes 9437188
  2.5 0.7 copy-start.2
  3.3 0.7 copy-start.3
  6.3 2.2 %copy-start = (bf16[16,64,2304]{2,1,0:T(8,128)(2,1)}, bf16[16,64,2304]{2,1,0:T(8,128)(2,1)S(1)}, u32[]{:S(2)}) copy-start(bf16[16,64,2304]{2,1,0:T(8,128)(2,1)S(1)} %pack.1) | copy-start | bytes 14155780
  8.5 66.7 %all-to-all-start = ((bf16[16,64,2304]{2,1,0:T(8,128)(2,1)}), bf16[16,64,2304]{2,1,0:T(8,128)(2,1)}, u32[]{:S(2)}, u32[]{:S(2)}) async-start(bf16[16,64,2304]{2,1,0:T(8,128)(2,1)} %copy-done), calls=%async_computation | async-start | bytes 9437184 | tf_op jit(solution)/shard_map/all_to_all | solution.py:195
  78.9 5.7 %collective-permute-start = (bf16[16,320,128]{2,1,0:T(8,128)(2,1)S(1)}, bf16[16,320,128]{2,1,0:T(8,128)(2,1)S(1)}, u32[]{:S(2)}, u32[]{:S(2)}) collective-permute-start(bf16[16,320,128]{2,1,0:T(8,128)(2,1)S(1)} %blocks.3), channel_id=1, source_target_pairs={{0,1},{1,0},{2,3},{3,2},{4,5},{5,4},{6,7},{7,6},{8,9},{9,8},{10,11... | collective-permute-start | bytes 3932168 | tf_op jit(solution)/shard_map/ppermute | solution.py:199
  86.0 23.5 %copy-start.4 = (s32[6,13]{1,0:T(8,128)S(1)}, s32[6,13]{1,0:T(8,128)}, u32[]{:S(2)}) copy-start(s32[6,13]{1,0:T(8,128)} %param.10) | copy-start | bytes 940
  86.0 23.6 %copy-start.5 = (s32[6,12]{1,0:T(8,128)S(1)}, s32[6,12]{1,0:T(8,128)}, u32[]{:S(2)}) copy-start(s32[6,12]{1,0:T(8,128)} %constant.30.clone) | copy-start | bytes 868
  86.0 72.4 %all-to-all-start.1 = ((bf16[16,320,128]{2,1,0:T(8,128)(2,1)}), bf16[16,320,128]{2,1,0:T(8,128)(2,1)S(1)}, u32[]{:S(2)}, u32[]{:S(2)}) async-start(bf16[16,320,128]{2,1,0:T(8,128)(2,1)} %add_convert_fusion), calls=%async_computation.1 | async-start | bytes 2621440 | tf_op jit(solution)/shard_map/all_to_all | solution.py:202
  158.5 11.1 %collective-permute-start.1 = (bf16[320,128]{1,0:T(8,128)(2,1)S(1)}, bf16[320,128]{1,0:T(8,128)(2,1)S(1)}, u32[]{:S(2)}, u32[]{:S(2)}) collective-permute-start(bf16[320,128]{1,0:T(8,128)(2,1)S(1)} %reduce_sum.22), channel_id=1, source_target_pairs={{0,0},{1,1},{2,2},{3,3},{4,4},{5,5},{6,6},{7,7},{8,32},{9,33},{10,... | collective-permute-start | bytes 245768 | tf_op jit(solution)/shard_map/ppermute | solution.py:204

commit v3 on v2

v3 whole, which is shorter than its diff:
```python
import functools
import math

import jax
import jax.numpy as jnp
import numpy as np
from jax import lax
from jax.experimental import pallas as pl
from jax.experimental.pallas import tpu as pltpu
from jax.sharding import Mesh
from jax.sharding import PartitionSpec as P

CELLS = 128
BRICK_Y = 2
BRICK_Z = 3
SLAB = BRICK_Y * BRICK_Z
WIDTH = SLAB * CELLS
AXES = ("zh", "zl", "yl", "yh", "x", "core")
SIZES = (4, 2, 2, 4, 4, 2)
GATHER = ("yl", "zl", "x")
REDUCE = ("zh", "yh")

NEXT_PAIRS = [
    ((y * 3 + z, 6 + first), (y * 3 + z, 7 + first))
    for z, firsts in ((0, (0, 3)), (1, (0, 2, 4)), (2, (1, 4)))
    for y in range(BRICK_Y)
    for first in firsts
]
OWN_PAIRS = [
    ((0, 3), (0, 4)),
    ((1, 4), (1, 5)),
    ((2, 4), (2, 5)),
    ((0, 1), (1, 2)),
    ((1, 3), (3, 4)),
    ((4, 5), None),
]
PAIRS = NEXT_PAIRS + OWN_PAIRS
ROWS = 16 * len(PAIRS)
SHARES = 16


def block_table():
    table = np.full((SLAB, 2 * SLAB), -1, np.int32)
    for at, pair in enumerate(PAIRS):
        for half, block in enumerate(pair):
            if block is not None:
                table[block] = 2 * at + half
    return table


def pack_kernel(freq_ref, surface_ref, picks_ref, panels_ref, out_ref, held, made, arrived, left, *, total_rows):
    rows, cells = held.shape
    pairs = made.shape[0]
    chunks = arrived.shape[0]
    width = cells // chunks

    def fetch(chunk):
        columns = pl.ds(chunk * width, width)
        return pltpu.make_async_copy(panels_ref.at[:, columns], held.at[:, columns], arrived.at[chunk])

    def store(pair):
        return pltpu.make_async_copy(made.at[pair], out_ref.at[pair], left.at[pair])

    for chunk in range(chunks):
        fetch(chunk).start()
    own_points = rows // 2
    first = lax.axis_index(("yh", "x", "core")) * own_points
    row = lax.broadcasted_iota(jnp.int32, (own_points, CELLS), 0)
    picked = jnp.zeros((own_points, CELLS), jnp.float32)
    for point in range(own_points):
        picked = jnp.where(row == point, surface_ref[picks_ref[first + point]], picked)
    scale = jnp.sqrt(picked * (freq_ref[0] * (1.0 / math.sqrt(total_rows))))
    scale = jnp.concatenate([scale, scale], axis=0)
    scale = jnp.concatenate([scale] * SLAB, axis=1)
    slabs = 2 * pairs
    for slab in range(slabs):
        if slab * chunks % slabs == 0:
            fetch(slab * chunks // slabs).wait()
        block = (held[:, slab * WIDTH : (slab + 1) * WIDTH].astype(jnp.float32) * scale).astype(jnp.bfloat16)
        made[slab // 2, :, slab % 2 * WIDTH : (slab % 2 + 1) * WIDTH] = block
        if slab % 2 == 0:
            made[(slab // 2 - 1) % pairs, :, 2 * WIDTH :] = block
            if slab > 0:
                store(slab // 2 - 1).start()
    store(pairs - 1).start()
    for pair in range(pairs):
        store(pair).wait()


def pack(panels, freq_weight, surface_weight, picks, total_rows):
    rows, cells = panels.shape
    pairs = cells // (2 * WIDTH)
    return pl.pallas_call(
        functools.partial(pack_kernel, total_rows=total_rows),
        in_specs=[
            pl.BlockSpec(memory_space=pltpu.SMEM),
            pl.BlockSpec(memory_space=pltpu.SMEM),
            pl.BlockSpec(memory_space=pltpu.SMEM),
            pl.BlockSpec(memory_space=pl.ANY),
        ],
        out_specs=pl.BlockSpec(memory_space=pl.ANY),
        out_shape=jax.ShapeDtypeStruct((pairs, rows, 3 * WIDTH), jnp.bfloat16),
        scratch_shapes=[
            pltpu.VMEM((rows, cells), jnp.bfloat16),
            pltpu.VMEM((pairs, rows, 3 * WIDTH), jnp.bfloat16),
            pltpu.SemaphoreType.DMA((8,)),
            pltpu.SemaphoreType.DMA((pairs,)),
        ],
        compiler_params=pltpu.CompilerParams(vmem_limit_bytes=54 * 1024 * 1024),
        name="pack",
    )(freq_weight, surface_weight, picks, panels)


def blocks_kernel(gathered_ref, out_ref, turned, *, own):
    core = lax.axis_index("core")
    start = (core if own else 1 - core) * WIDTH

    def columns(first, count):
        return gathered_ref[:, pl.ds(pl.multiple_of(start + first * CELLS, CELLS), count * CELLS)]

    for brick in range(SLAB):
        turned[brick * CELLS : (brick + 1) * CELLS, :] = columns(brick, 1).T

    def product(bricks, first, count):
        left = jnp.concatenate([turned[b * CELLS : (b + 1) * CELLS, :] for b in bricks], axis=0)
        made = jnp.dot(left, columns(first, count), preferred_element_type=jnp.float32)
        return {
            (b, first + n): made[m * CELLS : (m + 1) * CELLS, n * CELLS : (n + 1) * CELLS]
            for m, b in enumerate(bricks)
            for n in range(count)
        }

    def store(at, pair, made):
        parts = [
            made[b].reshape(SHARES, CELLS // SHARES, CELLS) if b is not None
            else jnp.zeros((SHARES, CELLS // SHARES, CELLS), jnp.float32)
            for b in pair
        ]
        out_ref[:, 16 * at : 16 * (at + 1), :] = jnp.concatenate(parts, axis=1).astype(jnp.bfloat16)

    for z, firsts in ((0, (0, 3)), (1, (0, 2, 4)), (2, (1, 4))):
        bricks = (z, 3 + z)
        for first in firsts:
            made = product(bricks, SLAB + first, 2)
            for at, pair in enumerate(PAIRS):
                if pair[0] in made:
                    store(at, pair, made)
    made = product((0, 1, 2), 3, 3)
    made.update({k: v for k, v in product((0, 1), 1, 2).items() if k in ((0, 1), (1, 2))})
    made.update({k: v for k, v in product((3, 4), 4, 2).items() if k in ((3, 4), (4, 5))})
    for at in range(len(NEXT_PAIRS), len(PAIRS)):
        store(at, PAIRS[at], made)


def blocks(gathered, own):
    rows = gathered.shape[0]
    return pl.pallas_call(
        functools.partial(blocks_kernel, own=own),
        in_specs=[pl.BlockSpec(memory_space=pltpu.VMEM)],
        out_specs=pl.BlockSpec(memory_space=pltpu.VMEM),
        out_shape=jax.ShapeDtypeStruct((SHARES, ROWS, CELLS), jnp.bfloat16),
        scratch_shapes=[pltpu.VMEM((WIDTH, rows), jnp.bfloat16)],
        compiler_params=pltpu.CompilerParams(vmem_limit_bytes=24 * 1024 * 1024),
        cost_estimate=pl.CostEstimate(
            flops=2 * 48 * CELLS * CELLS * rows, bytes_accessed=2 * rows * 2 * WIDTH + 2 * SHARES * ROWS * CELLS, transcendentals=0
        ),
        name="blocks",
    )(gathered)


def slots_kernel(index_ref, held_ref, out_ref):
    for b in range(out_ref.shape[0]):
        for k in range(out_ref.shape[1]):
            at = index_ref[b, k]
            block = held_ref[jnp.maximum(at, 0)]
            out_ref[b, k] = jnp.where(at >= 0, block, jnp.zeros_like(block))


def slots(held, index):
    share = held.shape[1]
    return pl.pallas_call(
        slots_kernel,
        in_specs=[pl.BlockSpec(memory_space=pltpu.SMEM), pl.BlockSpec(memory_space=pltpu.VMEM)],
        out_specs=pl.BlockSpec(memory_space=pltpu.VMEM),
        out_shape=jax.ShapeDtypeStruct((*index.shape, share, CELLS), jnp.bfloat16),
        compiler_params=pltpu.CompilerParams(vmem_limit_bytes=16 * 1024 * 1024),
        name="slots",
    )(index, held)


def owner_route():
    route = []
    for source in range(math.prod(SIZES)):
        zh, zl, yl, yh, x, core = (int(v) for v in np.unravel_index(source, SIZES))
        target = np.ravel_multi_index((zh, yh // 2, yh % 2, yl * 2 + zl, x, core), SIZES)
        route.append((source, int(target)))
    return route


def block_index(neighbours):
    slab = lax.axis_index(("yh", "x", "core"))
    relative = neighbours - slab * SLAB
    at = relative[:, :, None] == jnp.arange(2 * SLAB, dtype=jnp.int32)[None, None, :]
    at = at & (neighbours >= 0)[:, :, None]
    return jnp.sum(jnp.where(at, jnp.asarray(block_table() + 1)[:, None, :], 0), axis=2).astype(jnp.int32) - 1


def shards(panels, freq_weight, surface_weight, picks, neighbours):
    freq_count, parts, own_points, cells = panels.shape
    points = picks.shape[0]
    total_rows = parts * points * lax.axis_size(("zh", "zl", "yl"))
    rows = parts * own_points
    packed = pack(panels.reshape(rows, cells), freq_weight, surface_weight, picks, total_rows)
    gathered = lax.all_to_all(packed, GATHER, split_axis=0, concat_axis=0, tiled=True)
    gathered = gathered.reshape(-1, 3 * WIDTH)
    other = blocks(gathered, False)
    neighbours, other = lax.optimization_barrier((neighbours, other))
    arrived = lax.ppermute(other, "core", [(0, 1), (1, 0)])
    index = block_index(neighbours)
    own = blocks(gathered, True)
    partial = (own.astype(jnp.float32) + arrived.astype(jnp.float32)).astype(jnp.bfloat16)
    partial, index = lax.optimization_barrier((partial, index))
    spread = lax.all_to_all(partial, REDUCE, split_axis=0, concat_axis=0, tiled=True)
    held = jnp.sum(spread.astype(jnp.float32), axis=0).astype(jnp.bfloat16)
    held = lax.ppermute(held, AXES, owner_route())
    return slots(held.reshape(-1, CELLS // SHARES, CELLS), index)


def solution(mesh):
    fine = Mesh(mesh.devices.reshape(SIZES), AXES)
    freq, brick = ("zh", "zl", "yl"), ("yh", "x", "core")
    in_specs = (P(freq, None, brick, None), P(freq), P(), P(), P(brick, None))
    out_specs = P(brick, None, freq, None)
    return jax.shard_map(shards, mesh=fine, in_specs=in_specs, out_specs=out_specs, check_vma=False)
```

time: 172 us -> 144 us (0.84)
  the two profiles are of different devices: /device:TPU:68 before, /device:TPU:48 now
where the time goes in v3:
time: 144 us
  blocking collectives  118 us (82%)
  Pallas kernels  9.61 us (7%)
  waiting for transfers between devices  8.32 us (6%)
  starting transfers between devices  3.83 us (3%)
  local copies, waits for them, and re-layouts  2.55 us (2%)
    all_to_all x1, blocking collectives, shards(): lax.all_to_all(packed, GATHER, split_axis=0, concat_axis=0, tiled=True)  63.2 us
    all_to_all x1, blocking collectives, shards(): lax.all_to_all(partial, REDUCE, split_axis=0, concat_axis=0, tiled=True)  54.8 us
    ppermute x1, waiting for transfers between devices, shards(): held = lax.ppermute(held, AXES, owner_route())  8.31 us
    pallas_call x1, Pallas kernels, pack(): pl.pallas_call(functools.partial(pack_kernel, total_rows=total_rows), in_...  4.37 us
    pallas_call x2, Pallas kernels, blocks(): pl.pallas_call(functools.partial(blocks_kernel, own=own), in_specs=[pl.Bl...  3.8 us
  transfers between devices with their start and end apart: 2, of which 1 were waited for; matrix products, arithmetic and copies ran while one was open for 0% of the time, Pallas kernels for 1%

profile of v3, /device:TPU:48, one launch (start us, length us, event | category | flops | bytes accessed | tf_op | source)
XLA Modules:
  0.0 143.9 jit_solution(1677512569696680920)
XLA Ops:
  0.7 4.4 %pack.1 = bf16[16,64,2304]{2,1,0:T(8,128)(2,1)} custom-call(f32[1]{0:T(128)S(6)} %copy.7.freq_ref, f32[4096]{0:T(1024)} %surface_ref.1, s32[1024]{0:T(1024)} %picks_ref.1, bf16[64,24576]{1,0:T(8,128)(2,1)} %bitcast.6), custom_call_target="tpu_custom_call" | custom-call | tf_op jit(solution)/shard_map/pack/pallas_call | solution.py:93
  5.0 63.2 %all_to_all.10 = bf16[16,64,2304]{2,1,0:T(8,128)(2,1)S(1)} all-to-all(bf16[16,64,2304]{2,1,0:T(8,128)(2,1)} %pack.1), channel_id=1, replica_groups=mesh['zh'=4,'zl'=2,'yl'=2,'yh'=4,'x'=4,'core'=2] {'yl','zl','x'}, dimensions={0} | all-to-all | bytes 9437184 | tf_op jit(solution)/shard_map/all_to_all | solution.py:214
  68.2 0.0 copy-start
  68.2 0.0 copy-start.2
  68.2 0.0 copy-start.3
  68.2 1.9 %blocks.3 = bf16[16,320,128]{2,1,0:T(8,128)(2,1)S(1)} custom-call(bf16[1024,2304]{1,0:T(8,128)(2,1)S(1)} %bitcast.3), custom_call_target="tpu_custom_call" | custom-call | flops 1610612736 | bytes 4456448 | tf_op jit(solution)/shard_map/blocks/pallas_call | solution.py:157
  70.1 0.2 copy-done
  70.4 1.9 %collective-permute-start = (bf16[16,320,128]{2,1,0:T(8,128)(2,1)S(1)}, bf16[16,320,128]{2,1,0:T(8,128)(2,1)S(1)}, u32[]{:S(2)}, u32[]{:S(2)}) collective-permute-start(bf16[16,320,128]{2,1,0:T(8,128)(2,1)S(1)} %blocks.3), channel_id=1, source_target_pairs={{0,1},{1,0},{2,3},{3,2},{4,5},{5,4},{6,7},{7,6},{8,9},{9,8},{10,11... | collective-permute-start | bytes 3932168 | tf_op jit(solution)/shard_map/ppermute | solution.py:218
  72.3 0.0 copy-done.2
  72.3 0.0 copy-done.3
  72.3 0.3 select_reduce_fusion
  72.6 0.0 copy-start.1
  72.6 2.3 %copy-done.1 = bf16[16,64,2304]{2,1,0:T(8,128)(2,1)S(1)} copy-done((bf16[16,64,2304]{2,1,0:T(8,128)(2,1)S(1)}, bf16[16,64,2304]{2,1,0:T(8,128)(2,1)}, u32[]{:S(2)}) %copy-start.1) | copy-done | bytes 4718616
  74.9 1.9 %blocks.2 = bf16[16,320,128]{2,1,0:T(8,128)(2,1)S(1)} custom-call(bf16[1024,2304]{1,0:T(8,128)(2,1)S(1)} %bitcast.4), custom_call_target="tpu_custom_call" | custom-call | flops 1610612736 | bytes 4456448 | tf_op jit(solution)/shard_map/blocks/pallas_call | solution.py:157
  76.9 0.0 collective-permute-done
  76.9 0.3 add_convert_fusion
  77.2 54.8 %all_to_all.11 = bf16[16,320,128]{2,1,0:T(8,128)(2,1)S(1)} all-to-all(bf16[16,320,128]{2,1,0:T(8,128)(2,1)S(1)} %add_convert_fusion), channel_id=1, replica_groups=mesh['zh'=4,'zl'=2,'yl'=2,'yh'=4,'x'=4,'core'=2] {'zh','yh'}, dimensions={0} | all-to-all | bytes 2621440 | tf_op jit(solution)/shard_map/all_to_all | solution.py:223
  132.0 0.2 reduce_sum.22
  132.2 1.9 %collective-permute-start.1 = (bf16[320,128]{1,0:T(8,128)(2,1)S(1)}, bf16[320,128]{1,0:T(8,128)(2,1)S(1)}, u32[]{:S(2)}, u32[]{:S(2)}) collective-permute-start(bf16[320,128]{1,0:T(8,128)(2,1)S(1)} %reduce_sum.22), channel_id=1, source_target_pairs={{0,0},{1,1},{2,2},{3,3},{4,4},{5,5},{6,6},{7,7},{8,32},{9,33},{10,... | collective-permute-start | bytes 245768 | tf_op jit(solution)/shard_map/ppermute | solution.py:225
  134.1 8.3 %collective-permute-done.1 = bf16[320,128]{1,0:T(8,128)(2,1)S(1)} collective-permute-done((bf16[320,128]{1,0:T(8,128)(2,1)S(1)}, bf16[320,128]{1,0:T(8,128)(2,1)S(1)}, u32[]{:S(2)}, u32[]{:S(2)}) %collective-permute-start.1) | collective-permute-done | bytes 81952 | tf_op jit(solution)/shard_map/ppermute | solution.py:225
  142.5 1.4 %slots.1 = bf16[6,13,8,128]{3,2,1,0:T(8,128)(2,1)} custom-call(s32[6,13]{1,0:T(8,128)S(1)} %broadcast_add_fusion.index_ref, bf16[40,8,128]{2,1,0:T(8,128)(2,1)S(1)} %bitcast.5), custom_call_target="tpu_custom_call" | custom-call | tf_op jit(solution)/shard_map/slots/pallas_call | solution.py:181
  (3 shorter events, 0.0 us)
Async XLA Ops:
  68.2 2.1 %copy-start = (bf16[16,64,2304]{2,1,0:T(8,128)(2,1)}, bf16[16,64,2304]{2,1,0:T(8,128)(2,1)S(1)}, u32[]{:S(2)}) copy-start(bf16[16,64,2304]{2,1,0:T(8,128)(2,1)S(1)} %all_to_all.10) | copy-start | bytes 14155780
  68.2 4.0 %copy-start.2 = (s32[6,13]{1,0:T(8,128)S(1)}, s32[6,13]{1,0:T(8,128)}, u32[]{:S(2)}) copy-start(s32[6,13]{1,0:T(8,128)} %param.10) | copy-start | bytes 940
  68.2 4.1 %copy-start.3 = (s32[6,12]{1,0:T(8,128)S(1)}, s32[6,12]{1,0:T(8,128)}, u32[]{:S(2)}) copy-start(s32[6,12]{1,0:T(8,128)} %constant.28.clone) | copy-start | bytes 868
  70.4 6.5 %collective-permute-start = (bf16[16,320,128]{2,1,0:T(8,128)(2,1)S(1)}, bf16[16,320,128]{2,1,0:T(8,128)(2,1)S(1)}, u32[]{:S(2)}, u32[]{:S(2)}) collective-permute-start(bf16[16,320,128]{2,1,0:T(8,128)(2,1)S(1)} %blocks.3), channel_id=1, source_target_pairs={{0,1},{1,0},{2,3},{3,2},{4,5},{5,4},{6,7},{7,6},{8,9},{9,8},{10,11... | collective-permute-start | bytes 3932168 | tf_op jit(solution)/shard_map/ppermute | solution.py:218
  72.6 2.3 %copy-start.1 = (bf16[16,64,2304]{2,1,0:T(8,128)(2,1)S(1)}, bf16[16,64,2304]{2,1,0:T(8,128)(2,1)}, u32[]{:S(2)}) copy-start(bf16[16,64,2304]{2,1,0:T(8,128)(2,1)} %copy-done) | copy-start | bytes 14155780
  132.2 10.2 %collective-permute-start.1 = (bf16[320,128]{1,0:T(8,128)(2,1)S(1)}, bf16[320,128]{1,0:T(8,128)(2,1)S(1)}, u32[]{:S(2)}, u32[]{:S(2)}) collective-permute-start(bf16[320,128]{1,0:T(8,128)(2,1)S(1)} %reduce_sum.22), channel_id=1, source_target_pairs={{0,0},{1,1},{2,2},{3,3},{4,4},{5,5},{6,6},{7,7},{8,32},{9,33},{10,... | collective-permute-start | bytes 245768 | tf_op jit(solution)/shard_map/ppermute | solution.py:225

commit v4 on v3

--- a/solution.py
+++ b/solution.py
@@ -18,7 +18,6 @@
 AXES = ("zh", "zl", "yl", "yh", "x", "core")
 SIZES = (4, 2, 2, 4, 4, 2)
 GATHER = ("yl", "zl", "x")
-REDUCE = ("zh", "yh")
 
 NEXT_PAIRS = [
     ((y * 3 + z, 6 + first), (y * 3 + z, 7 + first))
@@ -160,7 +159,7 @@
         out_specs=pl.BlockSpec(memory_space=pltpu.VMEM),
         out_shape=jax.ShapeDtypeStruct((SHARES, ROWS, CELLS), jnp.bfloat16),
         scratch_shapes=[pltpu.VMEM((WIDTH, rows), jnp.bfloat16)],
-        compiler_params=pltpu.CompilerParams(vmem_limit_bytes=24 * 1024 * 1024),
+        compiler_params=pltpu.CompilerParams(vmem_limit_bytes=12 * 1024 * 1024),
         cost_estimate=pl.CostEstimate(
             flops=2 * 48 * CELLS * CELLS * rows, bytes_accessed=2 * rows * 2 * WIDTH + 2 * SHARES * ROWS * CELLS, transcendentals=0
         ),
@@ -188,13 +187,41 @@
     )(index, held)
 
 
+def places():
+    for device in range(math.prod(SIZES)):
+        yield device, dict(zip(AXES, (int(v) for v in np.unravel_index(device, SIZES))))
+
+
+def split_axes(core):
+    return ("yh", "zh") if core == 0 else ("zh", "yh")
+
+
+def split_groups(step):
+    groups = {}
+    for device, at in places():
+        axis = split_axes(at["core"])[step]
+        groups.setdefault(tuple(v for a, v in at.items() if a != axis), []).append(device)
+    return list(groups.values())
+
+
 def owner_route():
     route = []
-    for source in range(math.prod(SIZES)):
-        zh, zl, yl, yh, x, core = (int(v) for v in np.unravel_index(source, SIZES))
-        target = np.ravel_multi_index((zh, yh // 2, yh % 2, yl * 2 + zl, x, core), SIZES)
-        route.append((source, int(target)))
+    for source, at in places():
+        first, second = split_axes(at["core"])
+        share = at[first] * 4 + at[second]
+        owner = (share // 4, share // 2 % 2, share % 2, at["yl"] * 2 + at["zl"], at["x"], at["core"])
+        route.append((source, int(np.ravel_multi_index(owner, SIZES))))
     return route
+
+
+def summed_over(partial, step):
+    groups = split_groups(step)
+    parts = len(groups[0])
+    shape = partial.shape
+    partial = partial.reshape(parts, shape[0] // parts * shape[1], shape[2])
+    spread = lax.all_to_all(partial, AXES, split_axis=0, concat_axis=0, tiled=True, axis_index_groups=groups)
+    summed = jnp.sum(spread.astype(jnp.float32), axis=0).astype(jnp.bfloat16)
+    return summed.reshape(shape[0] // parts, *shape[1:])
 
 
 def block_index(neighbours):
@@ -220,8 +247,7 @@
     own = blocks(gathered, True)
     partial = (own.astype(jnp.float32) + arrived.astype(jnp.float32)).astype(jnp.bfloat16)
     partial, index = lax.optimization_barrier((partial, index))
-    spread = lax.all_to_all(partial, REDUCE, split_axis=0, concat_axis=0, tiled=True)
-    held = jnp.sum(spread.astype(jnp.float32), axis=0).astype(jnp.bfloat16)
+    held = summed_over(summed_over(partial, 0), 1)
     held = lax.ppermute(held, AXES, owner_route())
     return slots(held.reshape(-1, CELLS // SHARES, CELLS), index)
 

time: 144 us -> 136 us (0.944)
  the two profiles are of different devices: /device:TPU:48 before, /device:TPU:56 now
where the time goes in v4:
time: 136 us; the launch traced here: 135 us
  blocking collectives  108 us (79%)
  Pallas kernels  9.61 us (7%)
  waiting for transfers between devices  9.31 us (7%)
  starting transfers between devices  4.61 us (3%)
  local copies, waits for them, and re-layouts  2.56 us (2%)
    all_to_all x1, blocking collectives, shards(): lax.all_to_all(packed, GATHER, split_axis=0, concat_axis=0, tiled=True)  63.1 us
    all_to_all x2, blocking collectives, summed_over(): lax.all_to_all(partial, AXES, split_axis=0, concat_axis=0, tiled=True, ax...  44.4 us
    ppermute x1, waiting for transfers between devices, shards(): held = lax.ppermute(held, AXES, owner_route())  9.31 us
    pallas_call x1, Pallas kernels, pack(): pl.pallas_call(functools.partial(pack_kernel, total_rows=total_rows), in_...  4.37 us
    pallas_call x2, Pallas kernels, blocks(): pl.pallas_call(functools.partial(blocks_kernel, own=own), in_specs=[pl.Bl...  3.8 us
  transfers between devices with their start and end apart: 2, of which 1 were waited for; matrix products, arithmetic and copies ran while one was open for 0% of the time, Pallas kernels for 1%

profile of v4, /device:TPU:56, one launch (start us, length us, event | category | flops | bytes accessed | tf_op | source)
XLA Modules:
  0.0 135.4 jit_solution(4052353234910528338)
XLA Ops:
  0.7 4.4 %pack.1 = bf16[16,64,2304]{2,1,0:T(8,128)(2,1)} custom-call(f32[1]{0:T(128)S(6)} %copy.7.freq_ref, f32[4096]{0:T(1024)} %surface_ref.1, s32[1024]{0:T(1024)} %picks_ref.1, bf16[64,24576]{1,0:T(8,128)(2,1)} %bitcast.10), custom_call_target="tpu_custom_call" | custom-call | tf_op jit(solution)/shard_map/pack/pallas_call | solution.py:92
  5.0 63.1 %all_to_all.15 = bf16[16,64,2304]{2,1,0:T(8,128)(2,1)S(1)} all-to-all(bf16[16,64,2304]{2,1,0:T(8,128)(2,1)} %pack.1), channel_id=1, replica_groups=mesh['zh'=4,'zl'=2,'yl'=2,'yh'=4,'x'=4,'core'=2] {'yl','zl','x'}, dimensions={0} | all-to-all | bytes 9437184 | tf_op jit(solution)/shard_map/all_to_all | solution.py:241
  68.1 0.0 copy-start
  68.1 0.0 copy-start.2
  68.1 0.0 copy-start.3
  68.1 1.9 %blocks.3 = bf16[16,320,128]{2,1,0:T(8,128)(2,1)S(1)} custom-call(bf16[1024,2304]{1,0:T(8,128)(2,1)S(1)} %bitcast.6), custom_call_target="tpu_custom_call" | custom-call | flops 1610612736 | bytes 4456448 | tf_op jit(solution)/shard_map/blocks/pallas_call | solution.py:156
  70.0 0.2 copy-done
  70.2 1.9 %collective-permute-start = (bf16[16,320,128]{2,1,0:T(8,128)(2,1)S(1)}, bf16[16,320,128]{2,1,0:T(8,128)(2,1)S(1)}, u32[]{:S(2)}, u32[]{:S(2)}) collective-permute-start(bf16[16,320,128]{2,1,0:T(8,128)(2,1)S(1)} %blocks.3), channel_id=1, source_target_pairs={{0,1},{1,0},{2,3},{3,2},{4,5},{5,4},{6,7},{7,6},{8,9},{9,8},{10,11... | collective-permute-start | bytes 3932168 | tf_op jit(solution)/shard_map/ppermute | solution.py:245
  72.2 0.0 copy-done.2
  72.2 0.0 copy-done.3
  72.2 0.3 select_reduce_fusion
  72.5 0.0 copy-start.1
  72.5 2.3 %copy-done.1 = bf16[16,64,2304]{2,1,0:T(8,128)(2,1)S(1)} copy-done((bf16[16,64,2304]{2,1,0:T(8,128)(2,1)S(1)}, bf16[16,64,2304]{2,1,0:T(8,128)(2,1)}, u32[]{:S(2)}) %copy-start.1) | copy-done | bytes 4718616
  74.8 1.9 %blocks.2 = bf16[16,320,128]{2,1,0:T(8,128)(2,1)S(1)} custom-call(bf16[1024,2304]{1,0:T(8,128)(2,1)S(1)} %bitcast.7), custom_call_target="tpu_custom_call" | custom-call | flops 1610612736 | bytes 4456448 | tf_op jit(solution)/shard_map/blocks/pallas_call | solution.py:156
  76.7 0.0 collective-permute-done
  76.8 0.3 add_convert_fusion
  77.1 24.9 %all_to_all.16 = bf16[4,1280,128]{2,1,0:T(8,128)(2,1)S(1)} all-to-all(bf16[4,1280,128]{2,1,0:T(8,128)(2,1)S(1)} %bitcast.9), channel_id=1, replica_groups={{0,8,16,24},{1,129,257,385},{2,10,18,26},{3,131,259,387},{4,12,20,28},{..., dimensions={0} | all-to-all | bytes 2621440 | tf_op jit(solution)/shard_map/all_to_all | solution.py:222
  102.0 0.4 reduce_sum.34
  102.4 19.5 %all_to_all.17 = bf16[4,320,128]{2,1,0:T(8,128)(2,1)S(1)} all-to-all(bf16[4,320,128]{2,1,0:T(8,128)(2,1)S(1)} %bitcast.11), channel_id=1, replica_groups={{0,128,256,384},{1,9,17,25},{2,130,258,386},{3,11,19,27},{4,132,260,388..., dimensions={0} | all-to-all | bytes 655360 | tf_op jit(solution)/shard_map/all_to_all | solution.py:222
  122.0 2.7 %collective-permute-start.1 = (bf16[1,320,128]{2,1,0:T(8,128)(2,1)S(1)}, bf16[1,320,128]{2,1,0:T(8,128)(2,1)S(1)}, u32[]{:S(2)}, u32[]{:S(2)}) collective-permute-start(bf16[1,320,128]{2,1,0:T(8,128)(2,1)S(1)} %bitcast.12), channel_id=1, source_target_pairs={{0,0},{1,1},{2,2},{3,3},{4,4},{5,5},{6,6},{7,7},{8,128},{9,33},{10... | collective-permute-start | bytes 245768 | tf_op jit(solution)/shard_map/ppermute | solution.py:251
  124.7 9.3 %collective-permute-done.1 = bf16[1,320,128]{2,1,0:T(8,128)(2,1)S(1)} collective-permute-done((bf16[1,320,128]{2,1,0:T(8,128)(2,1)S(1)}, bf16[1,320,128]{2,1,0:T(8,128)(2,1)S(1)}, u32[]{:S(2)}, u32[]{:S(2)}) %collective-permute-start.1) | collective-permute-done | bytes 81952 | tf_op jit(solution)/shard_map/ppermute | solution.py:251
  134.0 1.4 %slots.1 = bf16[6,13,8,128]{3,2,1,0:T(8,128)(2,1)} custom-call(s32[6,13]{1,0:T(8,128)S(1)} %broadcast_add_fusion.index_ref, bf16[40,8,128]{2,1,0:T(8,128)(2,1)S(1)} %bitcast.8), custom_call_target="tpu_custom_call" | custom-call | tf_op jit(solution)/shard_map/slots/pallas_call | solution.py:180
  (4 shorter events, 0.1 us)
Async XLA Ops:
  68.1 2.1 %copy-start = (bf16[16,64,2304]{2,1,0:T(8,128)(2,1)}, bf16[16,64,2304]{2,1,0:T(8,128)(2,1)S(1)}, u32[]{:S(2)}) copy-start(bf16[16,64,2304]{2,1,0:T(8,128)(2,1)S(1)} %all_to_all.15) | copy-start | bytes 14155780
  68.1 4.0 %copy-start.2 = (s32[6,13]{1,0:T(8,128)S(1)}, s32[6,13]{1,0:T(8,128)}, u32[]{:S(2)}) copy-start(s32[6,13]{1,0:T(8,128)} %param.10) | copy-start | bytes 940
  68.1 4.1 %copy-start.3 = (s32[6,12]{1,0:T(8,128)S(1)}, s32[6,12]{1,0:T(8,128)}, u32[]{:S(2)}) copy-start(s32[6,12]{1,0:T(8,128)} %constant.29.clone) | copy-start | bytes 868
  70.2 6.5 %collective-permute-start = (bf16[16,320,128]{2,1,0:T(8,128)(2,1)S(1)}, bf16[16,320,128]{2,1,0:T(8,128)(2,1)S(1)}, u32[]{:S(2)}, u32[]{:S(2)}) collective-permute-start(bf16[16,320,128]{2,1,0:T(8,128)(2,1)S(1)} %blocks.3), channel_id=1, source_target_pairs={{0,1},{1,0},{2,3},{3,2},{4,5},{5,4},{6,7},{7,6},{8,9},{9,8},{10,11... | collective-permute-start | bytes 3932168 | tf_op jit(solution)/shard_map/ppermute | solution.py:245
  72.5 2.3 %copy-start.1 = (bf16[16,64,2304]{2,1,0:T(8,128)(2,1)S(1)}, bf16[16,64,2304]{2,1,0:T(8,128)(2,1)}, u32[]{:S(2)}) copy-start(bf16[16,64,2304]{2,1,0:T(8,128)(2,1)} %copy-done) | copy-start | bytes 14155780
  122.0 12.0 %collective-permute-start.1 = (bf16[1,320,128]{2,1,0:T(8,128)(2,1)S(1)}, bf16[1,320,128]{2,1,0:T(8,128)(2,1)S(1)}, u32[]{:S(2)}, u32[]{:S(2)}) collective-permute-start(bf16[1,320,128]{2,1,0:T(8,128)(2,1)S(1)} %bitcast.12), channel_id=1, source_target_pairs={{0,0},{1,1},{2,2},{3,3},{4,4},{5,5},{6,6},{7,7},{8,128},{9,33},{10... | collective-permute-start | bytes 245768 | tf_op jit(solution)/shard_map/ppermute | solution.py:251

commit v5 on v4

v5 whole, which is shorter than its diff:
```python
import functools
import math

import jax
import jax.numpy as jnp
import numpy as np
from jax import lax
from jax.experimental import pallas as pl
from jax.experimental.pallas import tpu as pltpu
from jax.sharding import Mesh
from jax.sharding import PartitionSpec as P

CELLS = 128
BRICK_Y = 2
BRICK_Z = 3
SLAB = BRICK_Y * BRICK_Z
WIDTH = SLAB * CELLS
AXES = ("zh", "zl", "yl", "yh", "x", "core")
SIZES = (4, 2, 2, 4, 4, 2)

NEXT_PAIRS = [
    ((y * 3 + z, 6 + first), (y * 3 + z, 7 + first))
    for z, firsts in ((0, (0, 3)), (1, (0, 2, 4)), (2, (1, 4)))
    for y in range(BRICK_Y)
    for first in firsts
]
OWN_PAIRS = [
    ((0, 3), (0, 4)),
    ((1, 4), (1, 5)),
    ((2, 4), (2, 5)),
    ((0, 1), (1, 2)),
    ((1, 3), (3, 4)),
    ((4, 5), None),
]
PAIRS = NEXT_PAIRS + OWN_PAIRS
ROWS = 16 * len(PAIRS)
SPLIT = 4
SHARES = SPLIT * SPLIT
OWNED = 2
SET = 2 * OWNED


def block_table():
    table = np.full((SLAB, 2 * SLAB), -1, np.int32)
    for at, pair in enumerate(PAIRS):
        for half, block in enumerate(pair):
            if block is not None:
                table[block] = 2 * at + half
    return table


def pack_kernel(freq_ref, surface_ref, picks_ref, panels_ref, out_ref, held, made, arrived, left, *, total_rows):
    rows, cells = held.shape
    sets = made.shape[0]
    chunks = arrived.shape[0]
    width = cells // chunks

    def fetch(chunk):
        columns = pl.ds(chunk * width, width)
        return pltpu.make_async_copy(panels_ref.at[:, columns], held.at[:, columns], arrived.at[chunk])

    def store(at):
        return pltpu.make_async_copy(made.at[at], out_ref.at[at], left.at[at])

    for chunk in range(chunks):
        fetch(chunk).start()
    own_points = rows // 2
    first = lax.axis_index(("yh", "x", "core")) * own_points
    row = lax.broadcasted_iota(jnp.int32, (own_points, CELLS), 0)
    picked = jnp.zeros((own_points, CELLS), jnp.float32)
    for point in range(own_points):
        picked = jnp.where(row == point, surface_ref[picks_ref[first + point]], picked)
    scale = jnp.sqrt(picked * (freq_ref[0] * (1.0 / math.sqrt(total_rows))))
    scale = jnp.concatenate([scale, scale], axis=0)
    scale = jnp.concatenate([scale] * SLAB, axis=1)
    slabs = SET * sets
    for slab in range(slabs):
        if slab * chunks % slabs == 0:
            fetch(slab * chunks // slabs).wait()
        block = (held[:, slab * WIDTH : (slab + 1) * WIDTH].astype(jnp.float32) * scale).astype(jnp.bfloat16)
        at, place = slab // SET, slab % SET
        made[at, :, place * WIDTH : (place + 1) * WIDTH] = block
        if place == 0:
            made[(at - 1) % sets, :, SET * WIDTH :] = block
            if at > 0:
                store(at - 1).start()
    store(sets - 1).start()
    for at in range(sets):
        store(at).wait()


def pack(panels, freq_weight, surface_weight, picks, total_rows):
    rows, cells = panels.shape
    sets = cells // (SET * WIDTH)
    return pl.pallas_call(
        functools.partial(pack_kernel, total_rows=total_rows),
        in_specs=[
            pl.BlockSpec(memory_space=pltpu.SMEM),
            pl.BlockSpec(memory_space=pltpu.SMEM),
            pl.BlockSpec(memory_space=pltpu.SMEM),
            pl.BlockSpec(memory_space=pl.ANY),
        ],
        out_specs=pl.BlockSpec(memory_space=pl.ANY),
        out_shape=jax.ShapeDtypeStruct((sets, rows, (SET + 1) * WIDTH), jnp.bfloat16),
        scratch_shapes=[
            pltpu.VMEM((rows, cells), jnp.bfloat16),
            pltpu.VMEM((sets, rows, (SET + 1) * WIDTH), jnp.bfloat16),
            pltpu.SemaphoreType.DMA((8,)),
            pltpu.SemaphoreType.DMA((sets,)),
        ],
        compiler_params=pltpu.CompilerParams(vmem_limit_bytes=54 * 1024 * 1024),
        name="pack",
    )(freq_weight, surface_weight, picks, panels)


def blocks_kernel(gathered_ref, out_ref, turned, *, own):
    core = lax.axis_index("core")
    holder = core if own else 1 - core
    for turn in range(OWNED):
        slab_blocks(gathered_ref, out_ref, turned, holder + OWNED * turn, turn)


def slab_blocks(gathered_ref, out_ref, turned, slab, turn):
    def columns(first, count):
        start = pl.multiple_of(slab * WIDTH + first * CELLS, CELLS)
        return gathered_ref[:, pl.ds(start, count * CELLS)]

    for brick in range(SLAB):
        turned[brick * CELLS : (brick + 1) * CELLS, :] = columns(brick, 1).T

    def product(bricks, first, count):
        left = jnp.concatenate([turned[b * CELLS : (b + 1) * CELLS, :] for b in bricks], axis=0)
        made = jnp.dot(left, columns(first, count), preferred_element_type=jnp.float32)
        return {
            (b, first + n): made[m * CELLS : (m + 1) * CELLS, n * CELLS : (n + 1) * CELLS]
            for m, b in enumerate(bricks)
            for n in range(count)
        }

    def store(at, pair, made):
        parts = [
            made[b].reshape(SHARES, CELLS // SHARES, CELLS) if b is not None
            else jnp.zeros((SHARES, CELLS // SHARES, CELLS), jnp.float32)
            for b in pair
        ]
        rows = jnp.concatenate(parts, axis=1).astype(jnp.bfloat16)
        out_ref[:, turn, :, 16 * at : 16 * (at + 1), :] = rows.reshape(SPLIT, SPLIT, 16, CELLS)

    for z, firsts in ((0, (0, 3)), (1, (0, 2, 4)), (2, (1, 4))):
        bricks = (z, 3 + z)
        for first in firsts:
            made = product(bricks, SLAB + first, 2)
            for at, pair in enumerate(PAIRS):
                if pair[0] in made:
                    store(at, pair, made)
    made = product((0, 1, 2), 3, 3)
    made.update({k: v for k, v in product((0, 1), 1, 2).items() if k in ((0, 1), (1, 2))})
    made.update({k: v for k, v in product((3, 4), 4, 2).items() if k in ((3, 4), (4, 5))})
    for at in range(len(NEXT_PAIRS), len(PAIRS)):
        store(at, PAIRS[at], made)


def blocks(gathered, own):
    rows = gathered.shape[0]
    return pl.pallas_call(
        functools.partial(blocks_kernel, own=own),
        in_specs=[pl.BlockSpec(memory_space=pltpu.VMEM)],
        out_specs=pl.BlockSpec(memory_space=pltpu.VMEM),
        out_shape=jax.ShapeDtypeStruct((SPLIT, OWNED, SPLIT, ROWS, CELLS), jnp.bfloat16),
        scratch_shapes=[pltpu.VMEM((WIDTH, rows), jnp.bfloat16)],
        compiler_params=pltpu.CompilerParams(vmem_limit_bytes=16 * 1024 * 1024),
        cost_estimate=pl.CostEstimate(
            flops=OWNED * 2 * 48 * CELLS * CELLS * rows,
            bytes_accessed=OWNED * (2 * rows * 2 * WIDTH + 2 * SHARES * ROWS * CELLS),
            transcendentals=0,
        ),
        name="blocks",
    )(gathered)


def slots_kernel(neighbours_ref, table_ref, held_ref, out_ref):
    first = lax.axis_index(("yh", "x", "core")) * SLAB
    for b in range(out_ref.shape[0]):
        for k in range(out_ref.shape[1]):
            neighbour = neighbours_ref[b, k]
            at = table_ref[b, jnp.clip(neighbour - first, 0, 2 * SLAB - 1)]
            block = held_ref[jnp.maximum(at, 0)]
            out_ref[b, k] = jnp.where((neighbour >= 0) & (at >= 0), block, jnp.zeros_like(block))


def slots(held, neighbours):
    share = held.shape[1]
    return pl.pallas_call(
        slots_kernel,
        in_specs=[
            pl.BlockSpec(memory_space=pltpu.SMEM),
            pl.BlockSpec(memory_space=pltpu.SMEM),
            pl.BlockSpec(memory_space=pltpu.VMEM),
        ],
        out_specs=pl.BlockSpec(memory_space=pltpu.VMEM),
        out_shape=jax.ShapeDtypeStruct((*neighbours.shape, share, CELLS), jnp.bfloat16),
        compiler_params=pltpu.CompilerParams(vmem_limit_bytes=16 * 1024 * 1024),
        name="slots",
    )(neighbours, jnp.asarray(block_table()), held)


def places():
    for device in range(math.prod(SIZES)):
        yield device, dict(zip(AXES, (int(v) for v in np.unravel_index(device, SIZES))))


def gather_groups():
    groups = {}
    for device, at in places():
        core = at["core"]
        y, z = at["yh"] * 2 + at["yl"], at["zh"] * 2 + at["zl"]
        pairs = ((at["x"] - core) % 4 // 2, (y - core) % 8 // 2, (z - core) % 8 // 2, core)
        groups.setdefault(pairs, []).append((at["yl"], at["zl"], at["x"] % 2, device))
    return [[member[-1] for member in sorted(group)] for group in groups.values()]


def split_axes(core):
    return ("yh", "zh") if core == 0 else ("zh", "yh")


def split_groups(step):
    groups = {}
    for device, at in places():
        half = at["x"] // 2
        first, second = split_axes(at["core"])
        if step == 0:
            rest, place = (at["zl"], at["yl"], at[second], at["x"] % 2, at["core"]), (at[first], half)
        else:
            rest, place = (at["zl"], at["yl"], at[first], at["x"], at["core"]), (at[second],)
        groups.setdefault(rest, []).append((place, device))
    return [[device for _, device in sorted(group)] for group in groups.values()]


def owner_route():
    route = []
    for source, at in places():
        first, second = split_axes(at["core"])
        share = at[first] * SPLIT + at[second]
        x = 2 * (at["x"] % 2) + at["x"] // 2
        owner = (share // 4, share // 2 % 2, share % 2, at["yl"] * 2 + at["zl"], x, at["core"])
        route.append((source, int(np.ravel_multi_index(owner, SIZES))))
    return route


def summed_over(partial, step):
    groups = split_groups(step)
    parts = len(groups[0])
    partial = partial.reshape(parts, -1, CELLS)
    spread = lax.all_to_all(partial, AXES, split_axis=0, concat_axis=0, tiled=True, axis_index_groups=groups)
    return jnp.sum(spread.astype(jnp.float32), axis=0).astype(jnp.bfloat16)


def shards(panels, freq_weight, surface_weight, picks, neighbours):
    freq_count, parts, own_points, cells = panels.shape
    points = picks.shape[0]
    total_rows = parts * points * lax.axis_size(("zh", "zl", "yl"))
    rows = parts * own_points
    packed = pack(panels.reshape(rows, cells), freq_weight, surface_weight, picks, total_rows)
    gathered = lax.all_to_all(packed, AXES, split_axis=0, concat_axis=0, tiled=True, axis_index_groups=gather_groups())
    gathered = gathered.reshape(-1, (SET + 1) * WIDTH)
    other = blocks(gathered, False)
    arrived = lax.ppermute(other, "core", [(0, 1), (1, 0)])
    own = blocks(gathered, True)
    partial = (own.astype(jnp.float32) + arrived.astype(jnp.float32)).astype(jnp.bfloat16)
    held = summed_over(summed_over(partial, 0), 1)
    held = lax.ppermute(held, AXES, owner_route())
    return slots(held.reshape(-1, CELLS // SHARES, CELLS), neighbours)


def solution(mesh):
    fine = Mesh(mesh.devices.reshape(SIZES), AXES)
    freq, brick = ("zh", "zl", "yl"), ("yh", "x", "core")
    in_specs = (P(freq, None, brick, None), P(freq), P(), P(), P(brick, None))
    out_specs = P(brick, None, freq, None)
    return jax.shard_map(shards, mesh=fine, in_specs=in_specs, out_specs=out_specs, check_vma=False)
```

time: 136 us -> 126 us (0.926)
  the two profiles are of different devices: /device:TPU:56 before, /device:TPU:114 now
where the time goes in v5:
time: 126 us; the launch traced here: 125 us
  blocking collectives  92.7 us (74%)
  waiting for transfers between devices  12.8 us (10%)
  Pallas kernels  9.7 us (8%)
  starting transfers between devices  8.07 us (6%)
  other arithmetic  1.5 us (1%)
    all_to_all x2, blocking collectives, summed_over(): lax.all_to_all(partial, AXES, split_axis=0, concat_axis=0, tiled=True, ax...  64.1 us
    all_to_all x1, blocking collectives, shards(): lax.all_to_all(packed, AXES, split_axis=0, concat_axis=0, tiled=True, axi...  28.6 us
    ppermute x1, waiting for transfers between devices, shards(): held = lax.ppermute(held, AXES, owner_route())  10.1 us
    ppermute x1, starting transfers between devices, shards(): held = lax.ppermute(held, AXES, owner_route())  4.89 us
    pallas_call x1, Pallas kernels, pack(): pl.pallas_call(functools.partial(pack_kernel, total_rows=total_rows), in_...  4.14 us
    pallas_call x2, Pallas kernels, blocks(): pl.pallas_call(functools.partial(blocks_kernel, own=own), in_specs=[pl.Bl...  3.79 us
    ppermute x1, starting transfers between devices, shards(): arrived = lax.ppermute(other, 'core', [(0, 1), (1, 0)])  3.18 us
    ppermute x1, waiting for transfers between devices, shards(): arrived = lax.ppermute(other, 'core', [(0, 1), (1, 0)])  2.61 us
  transfers between devices with their start and end apart: 2, of which 2 were waited for; matrix products, arithmetic and copies ran while one was open for 0% of the time, Pallas kernels for 2%

profile of v5, /device:TPU:114, one launch (start us, length us, event | category | flops | bytes accessed | tf_op | source)
XLA Modules:
  0.0 125.5 jit_solution(11317518777071027170)
XLA Ops:
  0.7 4.1 %pack.1 = bf16[8,64,3840]{2,1,0:T(8,128)(2,1)} custom-call(f32[1]{0:T(128)S(6)} %copy.7.freq_ref, f32[4096]{0:T(1024)} %surface_ref.1, s32[1024]{0:T(1024)} %picks_ref.1, bf16[64,24576]{1,0:T(8,128)(2,1)} %bitcast.9), custom_call_target="tpu_custom_call" | custom-call | tf_op jit(solution)/shard_map/pack/pallas_call | solution.py:95
  4.8 28.6 %all_to_all.15 = bf16[8,64,3840]{2,1,0:T(8,128)(2,1)S(1)} all-to-all(bf16[8,64,3840]{2,1,0:T(8,128)(2,1)} %pack.1), channel_id=1, replica_groups={{0,2,64,66,32,34,96,98},{1,7,449,455,57,63,505,511},{5,3,453,451,61,59,..., dimensions={0} | all-to-all | bytes 7864320 | tf_op jit(solution)/shard_map/all_to_all | solution.py:264
  33.4 1.9 %blocks.3 = bf16[4,2,4,320,128]{4,3,2,1,0:T(8,128)(2,1)S(1)} custom-call(bf16[512,3840]{1,0:T(8,128)(2,1)S(1)} %bitcast.5), custom_call_target="tpu_custom_call" | custom-call | flops 1610612736 | bytes 5767168 | tf_op jit(solution)/shard_map/blocks/pallas_call | solution.py:165
  35.3 3.2 %collective-permute-start = (bf16[4,2,4,320,128]{4,3,2,1,0:T(8,128)(2,1)S(1)}, bf16[4,2,4,320,128]{4,3,2,1,0:T(8,128)(2,1)S(1)}, u32[]{:S(2)}, u32[]{:S(2)}) collective-permute-start(bf16[4,2,4,320,128]{4,3,2,1,0:T(8,128)(2,1)S(1)} %blocks.3), channel_id=1, source_target_pairs={{0,1},{1,0},{2,3},{3,2},{4,5},{5,4},{6,7},{7,6},{8,9},{9,8},{10,11... | collective-permute-start | bytes 7864328 | tf_op jit(solution)/shard_map/ppermute | solution.py:267
  38.5 1.9 %blocks.2 = bf16[4,2,4,320,128]{4,3,2,1,0:T(8,128)(2,1)S(1)} custom-call(bf16[512,3840]{1,0:T(8,128)(2,1)S(1)} %bitcast.6), custom_call_target="tpu_custom_call" | custom-call | flops 1610612736 | bytes 5767168 | tf_op jit(solution)/shard_map/blocks/pallas_call | solution.py:165
  40.4 2.6 %collective-permute-done = bf16[4,2,4,320,128]{4,3,2,1,0:T(8,128)(2,1)S(1)} collective-permute-done((bf16[4,2,4,320,128]{4,3,2,1,0:T(8,128)(2,1)S(1)}, bf16[4,2,4,320,128]{4,3,2,1,0:T(8,128)(2,1)S(1)}, u32[]{:S(2)}, u32[]{:S(2)}) %collective-permute-start) | collective-permute-done | bytes 2621472 | tf_op jit(solution)/shard_map/ppermute | solution.py:267
  43.0 0.9 add_convert_fusion
  43.9 42.8 %all_to_all.16 = bf16[8,1280,128]{2,1,0:T(8,128)(2,1)S(1)} all-to-all(bf16[8,1280,128]{2,1,0:T(8,128)(2,1)S(1)} %bitcast.8), channel_id=1, replica_groups={{0,4,8,12,16,20,24,28},{1,5,129,133,257,261,385,389},{2,6,10,14,18,22,2..., dimensions={0} | all-to-all | bytes 5242880 | tf_op jit(solution)/shard_map/all_to_all | solution.py:254
  86.7 0.0 copy-start
  86.7 0.0 copy-start.1
  86.7 0.5 reduce_sum.24
  87.3 21.3 %all_to_all.17 = bf16[4,320,128]{2,1,0:T(8,128)(2,1)S(1)} all-to-all(bf16[4,320,128]{2,1,0:T(8,128)(2,1)S(1)} %bitcast.10), channel_id=1, replica_groups={{0,128,256,384},{1,9,17,25},{2,130,258,386},{3,11,19,27},{4,132,260,388..., dimensions={0} | all-to-all | bytes 655360 | tf_op jit(solution)/shard_map/all_to_all | solution.py:254
  108.6 4.9 %collective-permute-start.1 = (bf16[320,128]{1,0:T(8,128)(2,1)S(1)}, bf16[320,128]{1,0:T(8,128)(2,1)S(1)}, u32[]{:S(2)}, u32[]{:S(2)}) collective-permute-start(bf16[320,128]{1,0:T(8,128)(2,1)S(1)} %reduce_sum.25), channel_id=1, source_target_pairs={{0,0},{1,1},{2,4},{3,5},{4,2},{5,3},{6,6},{7,7},{8,128},{9,33},{10... | collective-permute-start | bytes 245768 | tf_op jit(solution)/shard_map/ppermute | solution.py:271
  113.5 10.1 %collective-permute-done.1 = bf16[320,128]{1,0:T(8,128)(2,1)S(1)} collective-permute-done((bf16[320,128]{1,0:T(8,128)(2,1)S(1)}, bf16[320,128]{1,0:T(8,128)(2,1)S(1)}, u32[]{:S(2)}, u32[]{:S(2)}) %collective-permute-start.1) | collective-permute-done | bytes 81952 | tf_op jit(solution)/shard_map/ppermute | solution.py:271
  123.7 0.0 copy-done
  123.7 0.0 copy-done.1
  123.7 1.8 %slots.1 = bf16[6,13,8,128]{3,2,1,0:T(8,128)(2,1)} custom-call(s32[6,13]{1,0:T(8,128)S(1)} %copy-done, s32[6,12]{1,0:T(8,128)S(1)} %copy-done.1, bf16[40,8,128]{2,1,0:T(8,128)(2,1)S(1)} %bitcast.7), custom_call_target="tpu_custom_call" | custom-call | tf_op jit(solution)/shard_map/slots/pallas_call | solution.py:193
  (1 shorter events, 0.0 us)
Async XLA Ops:
  35.3 7.7 %collective-permute-start = (bf16[4,2,4,320,128]{4,3,2,1,0:T(8,128)(2,1)S(1)}, bf16[4,2,4,320,128]{4,3,2,1,0:T(8,128)(2,1)S(1)}, u32[]{:S(2)}, u32[]{:S(2)}) collective-permute-start(bf16[4,2,4,320,128]{4,3,2,1,0:T(8,128)(2,1)S(1)} %blocks.3), channel_id=1, source_target_pairs={{0,1},{1,0},{2,3},{3,2},{4,5},{5,4},{6,7},{7,6},{8,9},{9,8},{10,11... | collective-permute-start | bytes 7864328 | tf_op jit(solution)/shard_map/ppermute | solution.py:267
  86.7 37.0 %copy-start = (s32[6,13]{1,0:T(8,128)S(1)}, s32[6,13]{1,0:T(8,128)}, u32[]{:S(2)}) copy-start(s32[6,13]{1,0:T(8,128)} %neighbours_ref.1) | copy-start | bytes 940
  86.7 37.0 %copy-start.1 = (s32[6,12]{1,0:T(8,128)S(1)}, s32[6,12]{1,0:T(8,128)}, u32[]{:S(2)}) copy-start(s32[6,12]{1,0:T(8,128)} %constant.6.clone.table_ref) | copy-start | bytes 868
  108.6 15.0 %collective-permute-start.1 = (bf16[320,128]{1,0:T(8,128)(2,1)S(1)}, bf16[320,128]{1,0:T(8,128)(2,1)S(1)}, u32[]{:S(2)}, u32[]{:S(2)}) collective-permute-start(bf16[320,128]{1,0:T(8,128)(2,1)S(1)} %reduce_sum.25), channel_id=1, source_target_pairs={{0,0},{1,1},{2,4},{3,5},{4,2},{5,3},{6,6},{7,7},{8,128},{9,33},{10... | collective-permute-start | bytes 245768 | tf_op jit(solution)/shard_map/ppermute | solution.py:271

commit v6 on v5

--- a/solution.py
+++ b/solution.py
@@ -49,7 +49,7 @@
     return table
 
 
-def pack_kernel(freq_ref, surface_ref, picks_ref, panels_ref, out_ref, held, made, arrived, left, *, total_rows):
+def pack_kernel(freq_ref, surface_hbm, picks_hbm, panels_ref, out_ref, surface_ref, picks_ref, held, made, small, arrived, left, *, total_rows):
     rows, cells = held.shape
     sets = made.shape[0]
     chunks = arrived.shape[0]
@@ -62,15 +62,23 @@
     def store(at):
         return pltpu.make_async_copy(made.at[at], out_ref.at[at], left.at[at])
 
+    points = [
+        pltpu.make_async_copy(surface_hbm, surface_ref, small.at[0]),
+        pltpu.make_async_copy(picks_hbm, picks_ref, small.at[1]),
+    ]
+    for copy in points:
+        copy.start()
     for chunk in range(chunks):
         fetch(chunk).start()
+    for copy in points:
+        copy.wait()
     own_points = rows // 2
     first = lax.axis_index(("yh", "x", "core")) * own_points
     row = lax.broadcasted_iota(jnp.int32, (own_points, CELLS), 0)
     picked = jnp.zeros((own_points, CELLS), jnp.float32)
     for point in range(own_points):
         picked = jnp.where(row == point, surface_ref[picks_ref[first + point]], picked)
-    scale = jnp.sqrt(picked * (freq_ref[0] * (1.0 / math.sqrt(total_rows))))
+    scale = jnp.sqrt(picked * (freq_ref[...] * (1.0 / math.sqrt(total_rows))))
     scale = jnp.concatenate([scale, scale], axis=0)
     scale = jnp.concatenate([scale] * SLAB, axis=1)
     slabs = SET * sets
@@ -95,32 +103,37 @@
     return pl.pallas_call(
         functools.partial(pack_kernel, total_rows=total_rows),
         in_specs=[
-            pl.BlockSpec(memory_space=pltpu.SMEM),
-            pl.BlockSpec(memory_space=pltpu.SMEM),
-            pl.BlockSpec(memory_space=pltpu.SMEM),
+            pl.BlockSpec(memory_space=pltpu.VMEM),
+            pl.BlockSpec(memory_space=pl.ANY),
+            pl.BlockSpec(memory_space=pl.ANY),
             pl.BlockSpec(memory_space=pl.ANY),
         ],
         out_specs=pl.BlockSpec(memory_space=pl.ANY),
         out_shape=jax.ShapeDtypeStruct((sets, rows, (SET + 1) * WIDTH), jnp.bfloat16),
         scratch_shapes=[
+            pltpu.SMEM(surface_weight.shape, jnp.float32),
+            pltpu.SMEM(picks.shape, jnp.int32),
             pltpu.VMEM((rows, cells), jnp.bfloat16),
             pltpu.VMEM((sets, rows, (SET + 1) * WIDTH), jnp.bfloat16),
+            pltpu.SemaphoreType.DMA((2,)),
             pltpu.SemaphoreType.DMA((8,)),
             pltpu.SemaphoreType.DMA((sets,)),
         ],
         compiler_params=pltpu.CompilerParams(vmem_limit_bytes=54 * 1024 * 1024),
         name="pack",
-    )(freq_weight, surface_weight, picks, panels)
+    )(freq_weight.reshape(1, 1), surface_weight, picks, panels)
 
 
 def blocks_kernel(gathered_ref, out_ref, turned, *, own):
     core = lax.axis_index("core")
     holder = core if own else 1 - core
     for turn in range(OWNED):
-        slab_blocks(gathered_ref, out_ref, turned, holder + OWNED * turn, turn)
-
-
-def slab_blocks(gathered_ref, out_ref, turned, slab, turn):
+        slab_blocks(gathered_ref, out_ref, turned, holder, turn)
+
+
+def slab_blocks(gathered_ref, out_ref, turned, holder, turn):
+    slab = holder + OWNED * turn
+
     def columns(first, count):
         start = pl.multiple_of(slab * WIDTH + first * CELLS, CELLS)
         return gathered_ref[:, pl.ds(start, count * CELLS)]
@@ -144,7 +157,11 @@
             for b in pair
         ]
         rows = jnp.concatenate(parts, axis=1).astype(jnp.bfloat16)
-        out_ref[:, turn, :, 16 * at : 16 * (at + 1), :] = rows.reshape(SPLIT, SPLIT, 16, CELLS)
+        for share in range(SHARES):
+            along_z, along_y = share // SPLIT, share % SPLIT
+            first = jnp.where(holder == 0, along_y, along_z)
+            second = jnp.where(holder == 0, along_z, along_y)
+            out_ref[first, turn, second, 16 * at : 16 * (at + 1), :] = rows[share]
 
     for z, firsts in ((0, (0, 3)), (1, (0, 2, 4)), (2, (1, 4))):
         bricks = (z, 3 + z)
@@ -239,8 +256,7 @@
 def owner_route():
     route = []
     for source, at in places():
-        first, second = split_axes(at["core"])
-        share = at[first] * SPLIT + at[second]
+        share = at["zh"] * SPLIT + at["yh"]
         x = 2 * (at["x"] % 2) + at["x"] // 2
         owner = (share // 4, share // 2 % 2, share % 2, at["yl"] * 2 + at["zl"], x, at["core"])
         route.append((source, int(np.ravel_multi_index(owner, SIZES))))

time: 126 us -> 125 us (level)
  the two profiles are of different devices: /device:TPU:114 before, /device:TPU:66 now
where the time goes in v6:
time: 125 us
  blocking collectives  96.7 us (77%)
  waiting for transfers between devices  12.3 us (10%)
  Pallas kernels  8.89 us (7%)
  starting transfers between devices  4.59 us (4%)
  other arithmetic  1.5 us (1%)
    all_to_all x2, blocking collectives, summed_over(): lax.all_to_all(partial, AXES, split_axis=0, concat_axis=0, tiled=True, ax...  63.9 us
    all_to_all x1, blocking collectives, shards(): lax.all_to_all(packed, AXES, split_axis=0, concat_axis=0, tiled=True, axi...  32.9 us
    ppermute x1, waiting for transfers between devices, shards(): held = lax.ppermute(held, AXES, owner_route())  9.36 us
    pallas_call x2, Pallas kernels, blocks(): pl.pallas_call(functools.partial(blocks_kernel, own=own), in_specs=[pl.Bl...  3.78 us
    pallas_call x1, Pallas kernels, pack(): pl.pallas_call(functools.partial(pack_kernel, total_rows=total_rows), in_...  3.33 us
    ppermute x1, waiting for transfers between devices, shards(): arrived = lax.ppermute(other, 'core', [(0, 1), (1, 0)])  2.97 us
    ppermute x1, starting transfers between devices, shards(): held = lax.ppermute(held, AXES, owner_route())  2.67 us
  transfers between devices with their start and end apart: 2, of which 2 were waited for; matrix products, arithmetic and copies ran while one was open for 0% of the time, Pallas kernels for 2%

profile of v6, /device:TPU:66, one launch (start us, length us, event | category | flops | bytes accessed | tf_op | source)
XLA Modules:
  0.0 124.8 jit_solution(7605264608842530269)
XLA Ops:
  0.7 3.3 %pack.1 = bf16[8,64,3840]{2,1,0:T(8,128)(2,1)} custom-call(f32[1,1]{1,0:T(1,128)} %bitcast.6.freq_ref, f32[4096]{0:T(1024)} %surface_hbm.1, s32[1024]{0:T(1024)} %picks_hbm.1, bf16[64,24576]{1,0:T(8,128)(2,1)} %bitcast.11), custom_call_target="tpu_custom_call" | custom-call | tf_op jit(solution)/shard_map/pack/pallas_call | solution.py:103
  4.0 32.9 %all_to_all.15 = bf16[8,64,3840]{2,1,0:T(8,128)(2,1)S(1)} all-to-all(bf16[8,64,3840]{2,1,0:T(8,128)(2,1)} %pack.1), channel_id=1, replica_groups={{0,2,64,66,32,34,96,98},{1,7,449,455,57,63,505,511},{5,3,453,451,61,59,..., dimensions={0} | all-to-all | bytes 7864320 | tf_op jit(solution)/shard_map/all_to_all | solution.py:280
  36.9 1.9 %blocks.3 = bf16[4,2,4,320,128]{4,3,2,1,0:T(8,128)(2,1)S(1)} custom-call(bf16[512,3840]{1,0:T(8,128)(2,1)S(1)} %bitcast.7), custom_call_target="tpu_custom_call" | custom-call | flops 1610612736 | bytes 5767168 | tf_op jit(solution)/shard_map/blocks/pallas_call | solution.py:182
  38.8 1.9 %collective-permute-start = (bf16[4,2,4,320,128]{4,3,2,1,0:T(8,128)(2,1)S(1)}, bf16[4,2,4,320,128]{4,3,2,1,0:T(8,128)(2,1)S(1)}, u32[]{:S(2)}, u32[]{:S(2)}) collective-permute-start(bf16[4,2,4,320,128]{4,3,2,1,0:T(8,128)(2,1)S(1)} %blocks.3), channel_id=1, source_target_pairs={{0,1},{1,0},{2,3},{3,2},{4,5},{5,4},{6,7},{7,6},{8,9},{9,8},{10,11... | collective-permute-start | bytes 7864328 | tf_op jit(solution)/shard_map/ppermute | solution.py:283
  40.7 1.9 %blocks.2 = bf16[4,2,4,320,128]{4,3,2,1,0:T(8,128)(2,1)S(1)} custom-call(bf16[512,3840]{1,0:T(8,128)(2,1)S(1)} %bitcast.8), custom_call_target="tpu_custom_call" | custom-call | flops 1610612736 | bytes 5767168 | tf_op jit(solution)/shard_map/blocks/pallas_call | solution.py:182
  42.6 3.0 %collective-permute-done = bf16[4,2,4,320,128]{4,3,2,1,0:T(8,128)(2,1)S(1)} collective-permute-done((bf16[4,2,4,320,128]{4,3,2,1,0:T(8,128)(2,1)S(1)}, bf16[4,2,4,320,128]{4,3,2,1,0:T(8,128)(2,1)S(1)}, u32[]{:S(2)}, u32[]{:S(2)}) %collective-permute-start) | collective-permute-done | bytes 2621472 | tf_op jit(solution)/shard_map/ppermute | solution.py:283
  45.6 0.9 add_convert_fusion
  46.5 42.6 %all_to_all.16 = bf16[8,1280,128]{2,1,0:T(8,128)(2,1)S(1)} all-to-all(bf16[8,1280,128]{2,1,0:T(8,128)(2,1)S(1)} %bitcast.10), channel_id=1, replica_groups={{0,4,8,12,16,20,24,28},{1,5,129,133,257,261,385,389},{2,6,10,14,18,22,2..., dimensions={0} | all-to-all | bytes 5242880 | tf_op jit(solution)/shard_map/all_to_all | solution.py:270
  89.1 0.0 copy-start
  89.1 0.0 copy-start.1
  89.1 0.5 reduce_sum.24
  89.6 21.2 %all_to_all.17 = bf16[4,320,128]{2,1,0:T(8,128)(2,1)S(1)} all-to-all(bf16[4,320,128]{2,1,0:T(8,128)(2,1)S(1)} %bitcast.12), channel_id=1, replica_groups={{0,128,256,384},{1,9,17,25},{2,130,258,386},{3,11,19,27},{4,132,260,388..., dimensions={0} | all-to-all | bytes 655360 | tf_op jit(solution)/shard_map/all_to_all | solution.py:270
  110.9 2.7 %collective-permute-start.1 = (bf16[320,128]{1,0:T(8,128)(2,1)S(1)}, bf16[320,128]{1,0:T(8,128)(2,1)S(1)}, u32[]{:S(2)}, u32[]{:S(2)}) collective-permute-start(bf16[320,128]{1,0:T(8,128)(2,1)S(1)} %reduce_sum.25), channel_id=1, source_target_pairs={{0,0},{1,1},{2,4},{3,5},{4,2},{5,3},{6,6},{7,7},{8,32},{9,33},{10,... | collective-permute-start | bytes 245768 | tf_op jit(solution)/shard_map/ppermute | solution.py:287
  113.6 9.4 %collective-permute-done.1 = bf16[320,128]{1,0:T(8,128)(2,1)S(1)} collective-permute-done((bf16[320,128]{1,0:T(8,128)(2,1)S(1)}, bf16[320,128]{1,0:T(8,128)(2,1)S(1)}, u32[]{:S(2)}, u32[]{:S(2)}) %collective-permute-start.1) | collective-permute-done | bytes 81952 | tf_op jit(solution)/shard_map/ppermute | solution.py:287
  123.0 0.0 copy-done
  123.0 0.0 copy-done.1
  123.0 1.8 %slots.1 = bf16[6,13,8,128]{3,2,1,0:T(8,128)(2,1)} custom-call(s32[6,13]{1,0:T(8,128)S(1)} %copy-done, s32[6,12]{1,0:T(8,128)S(1)} %copy-done.1, bf16[40,8,128]{2,1,0:T(8,128)(2,1)S(1)} %bitcast.9), custom_call_target="tpu_custom_call" | custom-call | tf_op jit(solution)/shard_map/slots/pallas_call | solution.py:210
  (1 shorter events, 0.0 us)
Async XLA Ops:
  38.8 6.8 %collective-permute-start = (bf16[4,2,4,320,128]{4,3,2,1,0:T(8,128)(2,1)S(1)}, bf16[4,2,4,320,128]{4,3,2,1,0:T(8,128)(2,1)S(1)}, u32[]{:S(2)}, u32[]{:S(2)}) collective-permute-start(bf16[4,2,4,320,128]{4,3,2,1,0:T(8,128)(2,1)S(1)} %blocks.3), channel_id=1, source_target_pairs={{0,1},{1,0},{2,3},{3,2},{4,5},{5,4},{6,7},{7,6},{8,9},{9,8},{10,11... | collective-permute-start | bytes 7864328 | tf_op jit(solution)/shard_map/ppermute | solution.py:283
  89.1 33.9 %copy-start = (s32[6,13]{1,0:T(8,128)S(1)}, s32[6,13]{1,0:T(8,128)}, u32[]{:S(2)}) copy-start(s32[6,13]{1,0:T(8,128)} %neighbours_ref.1) | copy-start | bytes 940
  89.1 33.9 %copy-start.1 = (s32[6,12]{1,0:T(8,128)S(1)}, s32[6,12]{1,0:T(8,128)}, u32[]{:S(2)}) copy-start(s32[6,12]{1,0:T(8,128)} %constant.6.clone.table_ref) | copy-start | bytes 868
  110.9 12.0 %collective-permute-start.1 = (bf16[320,128]{1,0:T(8,128)(2,1)S(1)}, bf16[320,128]{1,0:T(8,128)(2,1)S(1)}, u32[]{:S(2)}, u32[]{:S(2)}) collective-permute-start(bf16[320,128]{1,0:T(8,128)(2,1)S(1)} %reduce_sum.25), channel_id=1, source_target_pairs={{0,0},{1,1},{2,4},{3,5},{4,2},{5,3},{6,6},{7,7},{8,32},{9,33},{10,... | collective-permute-start | bytes 245768 | tf_op jit(solution)/shard_map/ppermute | solution.py:287

commit v7 on v6

--- a/solution.py
+++ b/solution.py
@@ -33,7 +33,7 @@
     ((4, 5), None),
 ]
 PAIRS = NEXT_PAIRS + OWN_PAIRS
-ROWS = 16 * len(PAIRS)
+ROWS = 8 * sum(block is not None for pair in PAIRS for block in pair)
 SPLIT = 4
 SHARES = SPLIT * SPLIT
 OWNED = 2
@@ -49,7 +49,7 @@
     return table
 
 
-def pack_kernel(freq_ref, surface_hbm, picks_hbm, panels_ref, out_ref, surface_ref, picks_ref, held, made, small, arrived, left, *, total_rows):
+def pack_kernel(freq_hbm, surface_hbm, picks_hbm, panels_ref, out_ref, freq_ref, surface_ref, picks_ref, held, made, small, arrived, left, *, total_rows):
     rows, cells = held.shape
     sets = made.shape[0]
     chunks = arrived.shape[0]
@@ -65,6 +65,7 @@
     points = [
         pltpu.make_async_copy(surface_hbm, surface_ref, small.at[0]),
         pltpu.make_async_copy(picks_hbm, picks_ref, small.at[1]),
+        pltpu.make_async_copy(freq_hbm, freq_ref, small.at[2]),
     ]
     for copy in points:
         copy.start()
@@ -78,7 +79,7 @@
     picked = jnp.zeros((own_points, CELLS), jnp.float32)
     for point in range(own_points):
         picked = jnp.where(row == point, surface_ref[picks_ref[first + point]], picked)
-    scale = jnp.sqrt(picked * (freq_ref[...] * (1.0 / math.sqrt(total_rows))))
+    scale = jnp.sqrt(picked * (freq_ref[0] * (1.0 / math.sqrt(total_rows))))
     scale = jnp.concatenate([scale, scale], axis=0)
     scale = jnp.concatenate([scale] * SLAB, axis=1)
     slabs = SET * sets
@@ -103,7 +104,7 @@
     return pl.pallas_call(
         functools.partial(pack_kernel, total_rows=total_rows),
         in_specs=[
-            pl.BlockSpec(memory_space=pltpu.VMEM),
+            pl.BlockSpec(memory_space=pl.ANY),
             pl.BlockSpec(memory_space=pl.ANY),
             pl.BlockSpec(memory_space=pl.ANY),
             pl.BlockSpec(memory_space=pl.ANY),
@@ -111,17 +112,18 @@
         out_specs=pl.BlockSpec(memory_space=pl.ANY),
         out_shape=jax.ShapeDtypeStruct((sets, rows, (SET + 1) * WIDTH), jnp.bfloat16),
         scratch_shapes=[
+            pltpu.SMEM(freq_weight.shape, jnp.float32),
             pltpu.SMEM(surface_weight.shape, jnp.float32),
             pltpu.SMEM(picks.shape, jnp.int32),
             pltpu.VMEM((rows, cells), jnp.bfloat16),
             pltpu.VMEM((sets, rows, (SET + 1) * WIDTH), jnp.bfloat16),
-            pltpu.SemaphoreType.DMA((2,)),
+            pltpu.SemaphoreType.DMA((3,)),
             pltpu.SemaphoreType.DMA((8,)),
             pltpu.SemaphoreType.DMA((sets,)),
         ],
         compiler_params=pltpu.CompilerParams(vmem_limit_bytes=54 * 1024 * 1024),
         name="pack",
-    )(freq_weight.reshape(1, 1), surface_weight, picks, panels)
+    )(freq_weight, surface_weight, picks, panels)
 
 
 def blocks_kernel(gathered_ref, out_ref, turned, *, own):
@@ -151,17 +153,13 @@
         }
 
     def store(at, pair, made):
-        parts = [
-            made[b].reshape(SHARES, CELLS // SHARES, CELLS) if b is not None
-            else jnp.zeros((SHARES, CELLS // SHARES, CELLS), jnp.float32)
-            for b in pair
-        ]
+        parts = [made[b].reshape(SHARES, CELLS // SHARES, CELLS) for b in pair if b is not None]
         rows = jnp.concatenate(parts, axis=1).astype(jnp.bfloat16)
         for share in range(SHARES):
             along_z, along_y = share // SPLIT, share % SPLIT
-            first = jnp.where(holder == 0, along_y, along_z)
-            second = jnp.where(holder == 0, along_z, along_y)
-            out_ref[first, turn, second, 16 * at : 16 * (at + 1), :] = rows[share]
+            first = jnp.where(holder == 0, along_z, along_y)
+            second = jnp.where(holder == 0, along_y, along_z)
+            out_ref[first, turn, second, 16 * at : 16 * at + rows.shape[1], :] = rows[share]
 
     for z, firsts in ((0, (0, 3)), (1, (0, 2, 4)), (2, (1, 4))):
         bricks = (z, 3 + z)
@@ -237,7 +235,7 @@
 
 
 def split_axes(core):
-    return ("yh", "zh") if core == 0 else ("zh", "yh")
+    return ("zh", "yh") if core == 0 else ("yh", "zh")
 
 
 def split_groups(step):

time: 125 us -> 121 us (0.968)
  the two profiles are of different devices: /device:TPU:66 before, /device:TPU:74 now
where the time goes in v7:
time: 121 us
  blocking collectives  92.7 us (77%)
  waiting for transfers between devices  10.4 us (9%)
  Pallas kernels  8.88 us (7%)
  starting transfers between devices  7.22 us (6%)
  other arithmetic  1.23 us (1%)
    all_to_all x2, blocking collectives, summed_over(): lax.all_to_all(partial, AXES, split_axis=0, concat_axis=0, tiled=True, ax...  60.9 us
    all_to_all x1, blocking collectives, shards(): lax.all_to_all(packed, AXES, split_axis=0, concat_axis=0, tiled=True, axi...  31.8 us
    ppermute x1, waiting for transfers between devices, shards(): held = lax.ppermute(held, AXES, owner_route())  7.53 us
    ppermute x1, starting transfers between devices, shards(): held = lax.ppermute(held, AXES, owner_route())  5.3 us
    pallas_call x2, Pallas kernels, blocks(): pl.pallas_call(functools.partial(blocks_kernel, own=own), in_specs=[pl.Bl...  3.77 us
    pallas_call x1, Pallas kernels, pack(): pl.pallas_call(functools.partial(pack_kernel, total_rows=total_rows), in_...  3.33 us
    ppermute x1, waiting for transfers between devices, shards(): arrived = lax.ppermute(other, 'core', [(0, 1), (1, 0)])  2.88 us
  transfers between devices with their start and end apart: 2, of which 2 were waited for; matrix products, arithmetic and copies ran while one was open for 0% of the time, Pallas kernels for 2%

profile of v7, /device:TPU:74, one launch (start us, length us, event | category | flops | bytes accessed | tf_op | source)
XLA Modules:
  0.0 121.2 jit_solution(5753158072877966418)
XLA Ops:
  0.7 3.3 %pack.1 = bf16[8,64,3840]{2,1,0:T(8,128)(2,1)} custom-call(f32[1]{0:T(128)S(6)} %copy.7.freq_hbm, f32[4096]{0:T(1024)} %surface_hbm.1, s32[1024]{0:T(1024)} %picks_hbm.1, bf16[64,24576]{1,0:T(8,128)(2,1)} %bitcast.9), custom_call_target="tpu_custom_call" | custom-call | tf_op jit(solution)/shard_map/pack/pallas_call | solution.py:104
  4.0 31.8 %all_to_all.15 = bf16[8,64,3840]{2,1,0:T(8,128)(2,1)S(1)} all-to-all(bf16[8,64,3840]{2,1,0:T(8,128)(2,1)} %pack.1), channel_id=1, replica_groups={{0,2,64,66,32,34,96,98},{1,7,449,455,57,63,505,511},{5,3,453,451,61,59,..., dimensions={0} | all-to-all | bytes 7864320 | tf_op jit(solution)/shard_map/all_to_all | solution.py:278
  35.8 1.9 %blocks.3 = bf16[4,2,4,312,128]{4,3,2,1,0:T(8,128)(2,1)S(1)} custom-call(bf16[512,3840]{1,0:T(8,128)(2,1)S(1)} %bitcast.5), custom_call_target="tpu_custom_call" | custom-call | flops 1610612736 | bytes 5701632 | tf_op jit(solution)/shard_map/blocks/pallas_call | solution.py:180
  37.7 1.9 %collective-permute-start = (bf16[4,2,4,312,128]{4,3,2,1,0:T(8,128)(2,1)S(1)}, bf16[4,2,4,312,128]{4,3,2,1,0:T(8,128)(2,1)S(1)}, u32[]{:S(2)}, u32[]{:S(2)}) collective-permute-start(bf16[4,2,4,312,128]{4,3,2,1,0:T(8,128)(2,1)S(1)} %blocks.3), channel_id=1, source_target_pairs={{0,1},{1,0},{2,3},{3,2},{4,5},{5,4},{6,7},{7,6},{8,9},{9,8},{10,11... | collective-permute-start | bytes 7667720 | tf_op jit(solution)/shard_map/ppermute | solution.py:281
  39.7 1.9 %blocks.2 = bf16[4,2,4,312,128]{4,3,2,1,0:T(8,128)(2,1)S(1)} custom-call(bf16[512,3840]{1,0:T(8,128)(2,1)S(1)} %bitcast.6), custom_call_target="tpu_custom_call" | custom-call | flops 1610612736 | bytes 5701632 | tf_op jit(solution)/shard_map/blocks/pallas_call | solution.py:180
  41.6 2.9 %collective-permute-done = bf16[4,2,4,312,128]{4,3,2,1,0:T(8,128)(2,1)S(1)} collective-permute-done((bf16[4,2,4,312,128]{4,3,2,1,0:T(8,128)(2,1)S(1)}, bf16[4,2,4,312,128]{4,3,2,1,0:T(8,128)(2,1)S(1)}, u32[]{:S(2)}, u32[]{:S(2)}) %collective-permute-start) | collective-permute-done | bytes 2555936 | tf_op jit(solution)/shard_map/ppermute | solution.py:281
  44.4 0.7 add_convert_fusion
  45.1 43.7 %all_to_all.16 = bf16[8,1248,128]{2,1,0:T(8,128)(2,1)S(1)} all-to-all(bf16[8,1248,128]{2,1,0:T(8,128)(2,1)S(1)} %bitcast.8), channel_id=1, replica_groups={{0,4,128,132,256,260,384,388},{1,5,9,13,17,21,25,29},{2,6,130,134,258,2..., dimensions={0} | all-to-all | bytes 5111808 | tf_op jit(solution)/shard_map/all_to_all | solution.py:268
  88.8 0.0 copy-start
  88.8 0.0 copy-start.1
  88.8 0.5 reduce_sum.24
  89.3 17.2 %all_to_all.17 = bf16[4,312,128]{2,1,0:T(8,128)(2,1)S(1)} all-to-all(bf16[4,312,128]{2,1,0:T(8,128)(2,1)S(1)} %bitcast.10), channel_id=1, replica_groups={{0,8,16,24},{1,129,257,385},{2,10,18,26},{3,131,259,387},{4,12,20,28},{..., dimensions={0} | all-to-all | bytes 638976 | tf_op jit(solution)/shard_map/all_to_all | solution.py:268
  106.6 5.3 %collective-permute-start.1 = (bf16[312,128]{1,0:T(8,128)(2,1)S(1)}, bf16[312,128]{1,0:T(8,128)(2,1)S(1)}, u32[]{:S(2)}, u32[]{:S(2)}) collective-permute-start(bf16[312,128]{1,0:T(8,128)(2,1)S(1)} %reduce_sum.25), channel_id=1, source_target_pairs={{0,0},{1,1},{2,4},{3,5},{4,2},{5,3},{6,6},{7,7},{8,32},{9,33},{10,... | collective-permute-start | bytes 239624 | tf_op jit(solution)/shard_map/ppermute | solution.py:285
  111.9 7.5 %collective-permute-done.1 = bf16[312,128]{1,0:T(8,128)(2,1)S(1)} collective-permute-done((bf16[312,128]{1,0:T(8,128)(2,1)S(1)}, bf16[312,128]{1,0:T(8,128)(2,1)S(1)}, u32[]{:S(2)}, u32[]{:S(2)}) %collective-permute-start.1) | collective-permute-done | bytes 79904 | tf_op jit(solution)/shard_map/ppermute | solution.py:285
  119.4 0.0 copy-done
  119.4 0.0 copy-done.1
  119.4 1.8 %slots.1 = bf16[6,13,8,128]{3,2,1,0:T(8,128)(2,1)} custom-call(s32[6,13]{1,0:T(8,128)S(1)} %copy-done, s32[6,12]{1,0:T(8,128)S(1)} %copy-done.1, bf16[39,8,128]{2,1,0:T(8,128)(2,1)S(1)} %bitcast.7), custom_call_target="tpu_custom_call" | custom-call | tf_op jit(solution)/shard_map/slots/pallas_call | solution.py:208
  (1 shorter events, 0.0 us)
Async XLA Ops:
  37.7 6.7 %collective-permute-start = (bf16[4,2,4,312,128]{4,3,2,1,0:T(8,128)(2,1)S(1)}, bf16[4,2,4,312,128]{4,3,2,1,0:T(8,128)(2,1)S(1)}, u32[]{:S(2)}, u32[]{:S(2)}) collective-permute-start(bf16[4,2,4,312,128]{4,3,2,1,0:T(8,128)(2,1)S(1)} %blocks.3), channel_id=1, source_target_pairs={{0,1},{1,0},{2,3},{3,2},{4,5},{5,4},{6,7},{7,6},{8,9},{9,8},{10,11... | collective-permute-start | bytes 7667720 | tf_op jit(solution)/shard_map/ppermute | solution.py:281
  88.8 30.6 %copy-start = (s32[6,13]{1,0:T(8,128)S(1)}, s32[6,13]{1,0:T(8,128)}, u32[]{:S(2)}) copy-start(s32[6,13]{1,0:T(8,128)} %neighbours_ref.1) | copy-start | bytes 940
  88.8 30.6 %copy-start.1 = (s32[6,12]{1,0:T(8,128)S(1)}, s32[6,12]{1,0:T(8,128)}, u32[]{:S(2)}) copy-start(s32[6,12]{1,0:T(8,128)} %constant.6.clone.table_ref) | copy-start | bytes 868
  106.6 12.8 %collective-permute-start.1 = (bf16[312,128]{1,0:T(8,128)(2,1)S(1)}, bf16[312,128]{1,0:T(8,128)(2,1)S(1)}, u32[]{:S(2)}, u32[]{:S(2)}) collective-permute-start(bf16[312,128]{1,0:T(8,128)(2,1)S(1)} %reduce_sum.25), channel_id=1, source_target_pairs={{0,0},{1,1},{2,4},{3,5},{4,2},{5,3},{6,6},{7,7},{8,32},{9,33},{10,... | collective-permute-start | bytes 239624 | tf_op jit(solution)/shard_map/ppermute | solution.py:285

commit v8 on v7

--- a/solution.py
+++ b/solution.py
@@ -156,7 +156,7 @@
         parts = [made[b].reshape(SHARES, CELLS // SHARES, CELLS) for b in pair if b is not None]
         rows = jnp.concatenate(parts, axis=1).astype(jnp.bfloat16)
         for share in range(SHARES):
-            along_z, along_y = share // SPLIT, share % SPLIT
+            along_z, along_y = share // SPLIT, share % 2 * 2 + share // 2 % 2
             first = jnp.where(holder == 0, along_z, along_y)
             second = jnp.where(holder == 0, along_y, along_z)
             out_ref[first, turn, second, 16 * at : 16 * at + rows.shape[1], :] = rows[share]
@@ -193,30 +193,44 @@
     )(gathered)
 
 
-def slots_kernel(neighbours_ref, table_ref, held_ref, out_ref):
+def index_kernel(neighbours_ref, table_ref, index_ref):
     first = lax.axis_index(("yh", "x", "core")) * SLAB
+    for b in range(index_ref.shape[0]):
+        for k in range(index_ref.shape[1]):
+            neighbour = neighbours_ref[b, k]
+            at = table_ref[b, jnp.clip(neighbour - first, 0, 2 * SLAB - 1)]
+            index_ref[b, k] = jnp.where(neighbour >= 0, at, -1)
+
+
+def block_index(neighbours):
+    return pl.pallas_call(
+        index_kernel,
+        in_specs=[pl.BlockSpec(memory_space=pltpu.SMEM)] * 2,
+        out_specs=pl.BlockSpec(memory_space=pltpu.SMEM),
+        out_shape=jax.ShapeDtypeStruct(neighbours.shape, jnp.int32),
+        compiler_params=pltpu.CompilerParams(vmem_limit_bytes=16 * 1024 * 1024),
+        name="block_index",
+    )(neighbours, jnp.asarray(block_table()))
+
+
+def slots_kernel(index_ref, held_ref, out_ref):
     for b in range(out_ref.shape[0]):
         for k in range(out_ref.shape[1]):
-            neighbour = neighbours_ref[b, k]
-            at = table_ref[b, jnp.clip(neighbour - first, 0, 2 * SLAB - 1)]
+            at = index_ref[b, k]
             block = held_ref[jnp.maximum(at, 0)]
-            out_ref[b, k] = jnp.where((neighbour >= 0) & (at >= 0), block, jnp.zeros_like(block))
-
-
-def slots(held, neighbours):
+            out_ref[b, k] = jnp.where(at >= 0, block, jnp.zeros_like(block))
+
+
+def slots(held, index):
     share = held.shape[1]
     return pl.pallas_call(
         slots_kernel,
-        in_specs=[
-            pl.BlockSpec(memory_space=pltpu.SMEM),
-            pl.BlockSpec(memory_space=pltpu.SMEM),
-            pl.BlockSpec(memory_space=pltpu.VMEM),
-        ],
+        in_specs=[pl.BlockSpec(memory_space=pltpu.SMEM), pl.BlockSpec(memory_space=pltpu.VMEM)],
         out_specs=pl.BlockSpec(memory_space=pltpu.VMEM),
-        out_shape=jax.ShapeDtypeStruct((*neighbours.shape, share, CELLS), jnp.bfloat16),
+        out_shape=jax.ShapeDtypeStruct((*index.shape, share, CELLS), jnp.bfloat16),
         compiler_params=pltpu.CompilerParams(vmem_limit_bytes=16 * 1024 * 1024),
         name="slots",
-    )(neighbours, jnp.asarray(block_table()), held)
+    )(index, held)
 
 
 def places():
@@ -254,7 +268,7 @@
 def owner_route():
     route = []
     for source, at in places():
-        share = at["zh"] * SPLIT + at["yh"]
+        share = at["zh"] * SPLIT + at["yh"] % 2 * 2 + at["yh"] // 2
         x = 2 * (at["x"] % 2) + at["x"] // 2
         owner = (share // 4, share // 2 % 2, share % 2, at["yl"] * 2 + at["zl"], x, at["core"])
         route.append((source, int(np.ravel_multi_index(owner, SIZES))))
@@ -282,8 +296,9 @@
     own = blocks(gathered, True)
     partial = (own.astype(jnp.float32) + arrived.astype(jnp.float32)).astype(jnp.bfloat16)
     held = summed_over(summed_over(partial, 0), 1)
+    neighbours, held = lax.optimization_barrier((neighbours, held))
     held = lax.ppermute(held, AXES, owner_route())
-    return slots(held.reshape(-1, CELLS // SHARES, CELLS), neighbours)
+    return slots(held.reshape(-1, CELLS // SHARES, CELLS), block_index(neighbours))
 
 
 def solution(mesh):

time: 121 us -> 121 us (level)
  the two profiles are of different devices: /device:TPU:74 before, /device:TPU:48 now
where the time goes in v8:
time: 121 us
  blocking collectives  86 us (71%)
  starting transfers between devices  13.3 us (11%)
  Pallas kernels  10.2 us (8%)
  waiting for transfers between devices  9.15 us (8%)
  other arithmetic  1.23 us (1%)
    all_to_all x2, blocking collectives, summed_over(): lax.all_to_all(partial, AXES, split_axis=0, concat_axis=0, tiled=True, ax...  55 us
    all_to_all x1, blocking collectives, shards(): lax.all_to_all(packed, AXES, split_axis=0, concat_axis=0, tiled=True, axi...  31 us
    ppermute x1, starting transfers between devices, shards(): arrived = lax.ppermute(other, 'core', [(0, 1), (1, 0)])  11.3 us
    ppermute x1, waiting for transfers between devices, shards(): held = lax.ppermute(held, AXES, owner_route())  6.64 us
    pallas_call x2, Pallas kernels, blocks(): pl.pallas_call(functools.partial(blocks_kernel, own=own), in_specs=[pl.Bl...  3.78 us
    pallas_call x1, Pallas kernels, pack(): pl.pallas_call(functools.partial(pack_kernel, total_rows=total_rows), in_...  3.33 us
    ppermute x1, waiting for transfers between devices, shards(): arrived = lax.ppermute(other, 'core', [(0, 1), (1, 0)])  2.52 us
  transfers between devices with their start and end apart: 2, of which 2 were waited for; matrix products, arithmetic and copies ran while one was open for 0% of the time, Pallas kernels for 3%

profile of v8, /device:TPU:48, one launch (start us, length us, event | category | flops | bytes accessed | tf_op | source)
XLA Modules:
  0.0 120.5 jit_solution(9494278494091709489)
XLA Ops:
  0.7 3.3 %pack.1 = bf16[8,64,3840]{2,1,0:T(8,128)(2,1)} custom-call(f32[1]{0:T(128)S(6)} %copy.7.freq_hbm, f32[4096]{0:T(1024)} %surface_hbm.1, s32[1024]{0:T(1024)} %picks_hbm.1, bf16[64,24576]{1,0:T(8,128)(2,1)} %bitcast.9), custom_call_target="tpu_custom_call" | custom-call | tf_op jit(solution)/shard_map/pack/pallas_call | solution.py:104
  4.0 31.0 %all_to_all.15 = bf16[8,64,3840]{2,1,0:T(8,128)(2,1)S(1)} all-to-all(bf16[8,64,3840]{2,1,0:T(8,128)(2,1)} %pack.1), channel_id=1, replica_groups={{0,2,64,66,32,34,96,98},{1,7,449,455,57,63,505,511},{5,3,453,451,61,59,..., dimensions={0} | all-to-all | bytes 7864320 | tf_op jit(solution)/shard_map/all_to_all | solution.py:292
  35.0 1.9 %blocks.3 = bf16[4,2,4,312,128]{4,3,2,1,0:T(8,128)(2,1)S(1)} custom-call(bf16[512,3840]{1,0:T(8,128)(2,1)S(1)} %bitcast.5), custom_call_target="tpu_custom_call" | custom-call | flops 1610612736 | bytes 5701632 | tf_op jit(solution)/shard_map/blocks/pallas_call | solution.py:180
  36.9 11.3 %collective-permute-start = (bf16[4,2,4,312,128]{4,3,2,1,0:T(8,128)(2,1)S(1)}, bf16[4,2,4,312,128]{4,3,2,1,0:T(8,128)(2,1)S(1)}, u32[]{:S(2)}, u32[]{:S(2)}) collective-permute-start(bf16[4,2,4,312,128]{4,3,2,1,0:T(8,128)(2,1)S(1)} %blocks.3), channel_id=1, source_target_pairs={{0,1},{1,0},{2,3},{3,2},{4,5},{5,4},{6,7},{7,6},{8,9},{9,8},{10,11... | collective-permute-start | bytes 7667720 | tf_op jit(solution)/shard_map/ppermute | solution.py:295
  48.2 1.9 %blocks.2 = bf16[4,2,4,312,128]{4,3,2,1,0:T(8,128)(2,1)S(1)} custom-call(bf16[512,3840]{1,0:T(8,128)(2,1)S(1)} %bitcast.6), custom_call_target="tpu_custom_call" | custom-call | flops 1610612736 | bytes 5701632 | tf_op jit(solution)/shard_map/blocks/pallas_call | solution.py:180
  50.1 2.5 %collective-permute-done = bf16[4,2,4,312,128]{4,3,2,1,0:T(8,128)(2,1)S(1)} collective-permute-done((bf16[4,2,4,312,128]{4,3,2,1,0:T(8,128)(2,1)S(1)}, bf16[4,2,4,312,128]{4,3,2,1,0:T(8,128)(2,1)S(1)}, u32[]{:S(2)}, u32[]{:S(2)}) %collective-permute-start) | collective-permute-done | bytes 2555936 | tf_op jit(solution)/shard_map/ppermute | solution.py:295
  52.6 0.7 add_convert_fusion
  53.3 41.4 %all_to_all.16 = bf16[8,1248,128]{2,1,0:T(8,128)(2,1)S(1)} all-to-all(bf16[8,1248,128]{2,1,0:T(8,128)(2,1)S(1)} %bitcast.8), channel_id=1, replica_groups={{0,4,128,132,256,260,384,388},{1,5,9,13,17,21,25,29},{2,6,130,134,258,2..., dimensions={0} | all-to-all | bytes 5111808 | tf_op jit(solution)/shard_map/all_to_all | solution.py:282
  94.7 0.0 copy-start
  94.7 0.0 copy-start.1
  94.7 0.5 reduce_sum.24
  95.3 13.5 %all_to_all.17 = bf16[4,312,128]{2,1,0:T(8,128)(2,1)S(1)} all-to-all(bf16[4,312,128]{2,1,0:T(8,128)(2,1)S(1)} %bitcast.10), channel_id=1, replica_groups={{0,8,16,24},{1,129,257,385},{2,10,18,26},{3,131,259,387},{4,12,20,28},{..., dimensions={0} | all-to-all | bytes 638976 | tf_op jit(solution)/shard_map/all_to_all | solution.py:282
  108.8 1.9 %collective-permute-start.1 = (bf16[312,128]{1,0:T(8,128)(2,1)S(1)}, bf16[312,128]{1,0:T(8,128)(2,1)S(1)}, u32[]{:S(2)}, u32[]{:S(2)}) collective-permute-start(bf16[312,128]{1,0:T(8,128)(2,1)S(1)} %reduce_sum.25), channel_id=1, source_target_pairs={{0,0},{1,1},{2,4},{3,5},{4,2},{5,3},{6,6},{7,7},{8,64},{9,65},{10,... | collective-permute-start | bytes 239624 | tf_op jit(solution)/shard_map/ppermute | solution.py:300
  110.8 0.0 copy-done
  110.8 0.0 copy-done.1
  110.8 1.6 %block_index.1.index_ref = s32[6,13]{1,0:T(8,128)S(1)} custom-call(s32[6,13]{1,0:T(8,128)S(1)} %copy-done, s32[6,12]{1,0:T(8,128)S(1)} %copy-done.1), custom_call_target="tpu_custom_call" | custom-call | tf_op jit(solution)/shard_map/block_index/pallas_call | solution.py:206
  112.4 6.6 %collective-permute-done.1 = bf16[312,128]{1,0:T(8,128)(2,1)S(1)} collective-permute-done((bf16[312,128]{1,0:T(8,128)(2,1)S(1)}, bf16[312,128]{1,0:T(8,128)(2,1)S(1)}, u32[]{:S(2)}, u32[]{:S(2)}) %collective-permute-start.1) | collective-permute-done | bytes 79904 | tf_op jit(solution)/shard_map/ppermute | solution.py:300
  119.1 1.4 %slots.1 = bf16[6,13,8,128]{3,2,1,0:T(8,128)(2,1)} custom-call(s32[6,13]{1,0:T(8,128)S(1)} %block_index.1.index_ref, bf16[39,8,128]{2,1,0:T(8,128)(2,1)S(1)} %bitcast.7), custom_call_target="tpu_custom_call" | custom-call | tf_op jit(solution)/shard_map/slots/pallas_call | solution.py:226
  (1 shorter events, 0.0 us)
Async XLA Ops:
  36.9 15.8 %collective-permute-start = (bf16[4,2,4,312,128]{4,3,2,1,0:T(8,128)(2,1)S(1)}, bf16[4,2,4,312,128]{4,3,2,1,0:T(8,128)(2,1)S(1)}, u32[]{:S(2)}, u32[]{:S(2)}) collective-permute-start(bf16[4,2,4,312,128]{4,3,2,1,0:T(8,128)(2,1)S(1)} %blocks.3), channel_id=1, source_target_pairs={{0,1},{1,0},{2,3},{3,2},{4,5},{5,4},{6,7},{7,6},{8,9},{9,8},{10,11... | collective-permute-start | bytes 7667720 | tf_op jit(solution)/shard_map/ppermute | solution.py:295
  94.7 16.0 %copy-start = (s32[6,13]{1,0:T(8,128)S(1)}, s32[6,13]{1,0:T(8,128)}, u32[]{:S(2)}) copy-start(s32[6,13]{1,0:T(8,128)} %neighbours_ref) | copy-start | bytes 940
  94.7 16.1 %copy-start.1 = (s32[6,12]{1,0:T(8,128)S(1)}, s32[6,12]{1,0:T(8,128)}, u32[]{:S(2)}) copy-start(s32[6,12]{1,0:T(8,128)} %constant.6.clone.table_ref) | copy-start | bytes 868
  108.8 10.2 %collective-permute-start.1 = (bf16[312,128]{1,0:T(8,128)(2,1)S(1)}, bf16[312,128]{1,0:T(8,128)(2,1)S(1)}, u32[]{:S(2)}, u32[]{:S(2)}) collective-permute-start(bf16[312,128]{1,0:T(8,128)(2,1)S(1)} %reduce_sum.25), channel_id=1, source_target_pairs={{0,0},{1,1},{2,4},{3,5},{4,2},{5,3},{6,6},{7,7},{8,64},{9,65},{10,... | collective-permute-start | bytes 239624 | tf_op jit(solution)/shard_map/ppermute | solution.py:300

commit v9 on v8

--- a/solution.py
+++ b/solution.py
@@ -168,9 +168,9 @@
             for at, pair in enumerate(PAIRS):
                 if pair[0] in made:
                     store(at, pair, made)
-    made = product((0, 1, 2), 3, 3)
-    made.update({k: v for k, v in product((0, 1), 1, 2).items() if k in ((0, 1), (1, 2))})
-    made.update({k: v for k, v in product((3, 4), 4, 2).items() if k in ((3, 4), (4, 5))})
+    made = {}
+    for bricks, first in (((0, 1), 3), ((1, 2), 4), ((0, 1), 1), ((3, 4), 4)):
+        made.update({block: value for block, value in product(bricks, first, 2).items() if block not in made})
     for at in range(len(NEXT_PAIRS), len(PAIRS)):
         store(at, PAIRS[at], made)
 
@@ -185,7 +185,7 @@
         scratch_shapes=[pltpu.VMEM((WIDTH, rows), jnp.bfloat16)],
         compiler_params=pltpu.CompilerParams(vmem_limit_bytes=16 * 1024 * 1024),
         cost_estimate=pl.CostEstimate(
-            flops=OWNED * 2 * 48 * CELLS * CELLS * rows,
+            flops=OWNED * 2 * 44 * CELLS * CELLS * rows,
             bytes_accessed=OWNED * (2 * rows * 2 * WIDTH + 2 * SHARES * ROWS * CELLS),
             transcendentals=0,
         ),

time: 121 us -> 121 us (level)
  no operation moved by 1% of the time
where the time goes in v9:
time: 121 us; the launch traced here: 120 us
  blocking collectives  86 us (71%)
  starting transfers between devices  13.3 us (11%)
  Pallas kernels  9.91 us (8%)
  waiting for transfers between devices  9.28 us (8%)
  other arithmetic  1.23 us (1%)
    all_to_all x2, blocking collectives, summed_over(): lax.all_to_all(partial, AXES, split_axis=0, concat_axis=0, tiled=True, ax...  55 us
    all_to_all x1, blocking collectives, shards(): lax.all_to_all(packed, AXES, split_axis=0, concat_axis=0, tiled=True, axi...  31 us
    ppermute x1, starting transfers between devices, shards(): arrived = lax.ppermute(other, 'core', [(0, 1), (1, 0)])  11.4 us
    ppermute x1, waiting for transfers between devices, shards(): held = lax.ppermute(held, AXES, owner_route())  6.64 us
    pallas_call x2, Pallas kernels, blocks(): pl.pallas_call(functools.partial(blocks_kernel, own=own), in_specs=[pl.Bl...  3.51 us
    pallas_call x1, Pallas kernels, pack(): pl.pallas_call(functools.partial(pack_kernel, total_rows=total_rows), in_...  3.33 us
    ppermute x1, waiting for transfers between devices, shards(): arrived = lax.ppermute(other, 'core', [(0, 1), (1, 0)])  2.65 us
  transfers between devices with their start and end apart: 2, of which 2 were waited for; matrix products, arithmetic and copies ran while one was open for 0% of the time, Pallas kernels for 3%

profile of v9, /device:TPU:48, one launch (start us, length us, event | category | flops | bytes accessed | tf_op | source)
XLA Modules:
  0.0 120.4 jit_solution(12690691010277354573)
XLA Ops:
  0.7 3.3 %pack.1 = bf16[8,64,3840]{2,1,0:T(8,128)(2,1)} custom-call(f32[1]{0:T(128)S(6)} %copy.7.freq_hbm, f32[4096]{0:T(1024)} %surface_hbm.1, s32[1024]{0:T(1024)} %picks_hbm.1, bf16[64,24576]{1,0:T(8,128)(2,1)} %bitcast.9), custom_call_target="tpu_custom_call" | custom-call | tf_op jit(solution)/shard_map/pack/pallas_call | solution.py:104
  4.0 31.0 %all_to_all.15 = bf16[8,64,3840]{2,1,0:T(8,128)(2,1)S(1)} all-to-all(bf16[8,64,3840]{2,1,0:T(8,128)(2,1)} %pack.1), channel_id=1, replica_groups={{0,2,64,66,32,34,96,98},{1,7,449,455,57,63,505,511},{5,3,453,451,61,59,..., dimensions={0} | all-to-all | bytes 7864320 | tf_op jit(solution)/shard_map/all_to_all | solution.py:292
  35.0 1.7 %blocks.3 = bf16[4,2,4,312,128]{4,3,2,1,0:T(8,128)(2,1)S(1)} custom-call(bf16[512,3840]{1,0:T(8,128)(2,1)S(1)} %bitcast.5), custom_call_target="tpu_custom_call" | custom-call | flops 1476395008 | bytes 5701632 | tf_op jit(solution)/shard_map/blocks/pallas_call | solution.py:180
  36.7 11.4 %collective-permute-start = (bf16[4,2,4,312,128]{4,3,2,1,0:T(8,128)(2,1)S(1)}, bf16[4,2,4,312,128]{4,3,2,1,0:T(8,128)(2,1)S(1)}, u32[]{:S(2)}, u32[]{:S(2)}) collective-permute-start(bf16[4,2,4,312,128]{4,3,2,1,0:T(8,128)(2,1)S(1)} %blocks.3), channel_id=1, source_target_pairs={{0,1},{1,0},{2,3},{3,2},{4,5},{5,4},{6,7},{7,6},{8,9},{9,8},{10,11... | collective-permute-start | bytes 7667720 | tf_op jit(solution)/shard_map/ppermute | solution.py:295
  48.1 1.8 %blocks.2 = bf16[4,2,4,312,128]{4,3,2,1,0:T(8,128)(2,1)S(1)} custom-call(bf16[512,3840]{1,0:T(8,128)(2,1)S(1)} %bitcast.6), custom_call_target="tpu_custom_call" | custom-call | flops 1476395008 | bytes 5701632 | tf_op jit(solution)/shard_map/blocks/pallas_call | solution.py:180
  49.9 2.6 %collective-permute-done = bf16[4,2,4,312,128]{4,3,2,1,0:T(8,128)(2,1)S(1)} collective-permute-done((bf16[4,2,4,312,128]{4,3,2,1,0:T(8,128)(2,1)S(1)}, bf16[4,2,4,312,128]{4,3,2,1,0:T(8,128)(2,1)S(1)}, u32[]{:S(2)}, u32[]{:S(2)}) %collective-permute-start) | collective-permute-done | bytes 2555936 | tf_op jit(solution)/shard_map/ppermute | solution.py:295
  52.5 0.7 add_convert_fusion
  53.2 41.4 %all_to_all.16 = bf16[8,1248,128]{2,1,0:T(8,128)(2,1)S(1)} all-to-all(bf16[8,1248,128]{2,1,0:T(8,128)(2,1)S(1)} %bitcast.8), channel_id=1, replica_groups={{0,4,128,132,256,260,384,388},{1,5,9,13,17,21,25,29},{2,6,130,134,258,2..., dimensions={0} | all-to-all | bytes 5111808 | tf_op jit(solution)/shard_map/all_to_all | solution.py:282
  94.6 0.0 copy-start
  94.6 0.0 copy-start.1
  94.6 0.5 reduce_sum.24
  95.1 13.5 %all_to_all.17 = bf16[4,312,128]{2,1,0:T(8,128)(2,1)S(1)} all-to-all(bf16[4,312,128]{2,1,0:T(8,128)(2,1)S(1)} %bitcast.10), channel_id=1, replica_groups={{0,8,16,24},{1,129,257,385},{2,10,18,26},{3,131,259,387},{4,12,20,28},{..., dimensions={0} | all-to-all | bytes 638976 | tf_op jit(solution)/shard_map/all_to_all | solution.py:282
  108.7 1.9 %collective-permute-start.1 = (bf16[312,128]{1,0:T(8,128)(2,1)S(1)}, bf16[312,128]{1,0:T(8,128)(2,1)S(1)}, u32[]{:S(2)}, u32[]{:S(2)}) collective-permute-start(bf16[312,128]{1,0:T(8,128)(2,1)S(1)} %reduce_sum.25), channel_id=1, source_target_pairs={{0,0},{1,1},{2,4},{3,5},{4,2},{5,3},{6,6},{7,7},{8,64},{9,65},{10,... | collective-permute-start | bytes 239624 | tf_op jit(solution)/shard_map/ppermute | solution.py:300
  110.7 0.0 copy-done
  110.7 0.0 copy-done.1
  110.7 1.6 %block_index.1.index_ref = s32[6,13]{1,0:T(8,128)S(1)} custom-call(s32[6,13]{1,0:T(8,128)S(1)} %copy-done, s32[6,12]{1,0:T(8,128)S(1)} %copy-done.1), custom_call_target="tpu_custom_call" | custom-call | tf_op jit(solution)/shard_map/block_index/pallas_call | solution.py:206
  112.3 6.6 %collective-permute-done.1 = bf16[312,128]{1,0:T(8,128)(2,1)S(1)} collective-permute-done((bf16[312,128]{1,0:T(8,128)(2,1)S(1)}, bf16[312,128]{1,0:T(8,128)(2,1)S(1)}, u32[]{:S(2)}, u32[]{:S(2)}) %collective-permute-start.1) | collective-permute-done | bytes 79904 | tf_op jit(solution)/shard_map/ppermute | solution.py:300
  118.9 1.4 %slots.1 = bf16[6,13,8,128]{3,2,1,0:T(8,128)(2,1)} custom-call(s32[6,13]{1,0:T(8,128)S(1)} %block_index.1.index_ref, bf16[39,8,128]{2,1,0:T(8,128)(2,1)S(1)} %bitcast.7), custom_call_target="tpu_custom_call" | custom-call | tf_op jit(solution)/shard_map/slots/pallas_call | solution.py:226
  (1 shorter events, 0.0 us)
Async XLA Ops:
  36.7 15.8 %collective-permute-start = (bf16[4,2,4,312,128]{4,3,2,1,0:T(8,128)(2,1)S(1)}, bf16[4,2,4,312,128]{4,3,2,1,0:T(8,128)(2,1)S(1)}, u32[]{:S(2)}, u32[]{:S(2)}) collective-permute-start(bf16[4,2,4,312,128]{4,3,2,1,0:T(8,128)(2,1)S(1)} %blocks.3), channel_id=1, source_target_pairs={{0,1},{1,0},{2,3},{3,2},{4,5},{5,4},{6,7},{7,6},{8,9},{9,8},{10,11... | collective-permute-start | bytes 7667720 | tf_op jit(solution)/shard_map/ppermute | solution.py:295
  94.6 16.0 %copy-start = (s32[6,13]{1,0:T(8,128)S(1)}, s32[6,13]{1,0:T(8,128)}, u32[]{:S(2)}) copy-start(s32[6,13]{1,0:T(8,128)} %neighbours_ref) | copy-start | bytes 940
  94.6 16.1 %copy-start.1 = (s32[6,12]{1,0:T(8,128)S(1)}, s32[6,12]{1,0:T(8,128)}, u32[]{:S(2)}) copy-start(s32[6,12]{1,0:T(8,128)} %constant.6.clone.table_ref) | copy-start | bytes 868
  108.7 10.2 %collective-permute-start.1 = (bf16[312,128]{1,0:T(8,128)(2,1)S(1)}, bf16[312,128]{1,0:T(8,128)(2,1)S(1)}, u32[]{:S(2)}, u32[]{:S(2)}) collective-permute-start(bf16[312,128]{1,0:T(8,128)(2,1)S(1)} %reduce_sum.25), channel_id=1, source_target_pairs={{0,0},{1,1},{2,4},{3,5},{4,2},{5,3},{6,6},{7,7},{8,64},{9,65},{10,... | collective-permute-start | bytes 239624 | tf_op jit(solution)/shard_map/ppermute | solution.py:300

commit v10 on v9

--- a/solution.py
+++ b/solution.py
@@ -59,8 +59,9 @@
         columns = pl.ds(chunk * width, width)
         return pltpu.make_async_copy(panels_ref.at[:, columns], held.at[:, columns], arrived.at[chunk])
 
-    def store(at):
-        return pltpu.make_async_copy(made.at[at], out_ref.at[at], left.at[at])
+    def store(at, part):
+        columns = pl.ds(0, OWNED * WIDTH) if part == 0 else pl.ds(OWNED * WIDTH, (SET + 1 - OWNED) * WIDTH)
+        return pltpu.make_async_copy(made.at[at, :, columns], out_ref.at[at, :, columns], left.at[at, part])
 
     points = [
         pltpu.make_async_copy(surface_hbm, surface_ref, small.at[0]),
@@ -92,10 +93,13 @@
         if place == 0:
             made[(at - 1) % sets, :, SET * WIDTH :] = block
             if at > 0:
-                store(at - 1).start()
-    store(sets - 1).start()
+                store(at - 1, 1).start()
+        elif place == OWNED - 1:
+            store(at, 0).start()
+    store(sets - 1, 1).start()
     for at in range(sets):
-        store(at).wait()
+        store(at, 0).wait()
+        store(at, 1).wait()
 
 
 def pack(panels, freq_weight, surface_weight, picks, total_rows):
@@ -118,8 +122,8 @@
             pltpu.VMEM((rows, cells), jnp.bfloat16),
             pltpu.VMEM((sets, rows, (SET + 1) * WIDTH), jnp.bfloat16),
             pltpu.SemaphoreType.DMA((3,)),
-            pltpu.SemaphoreType.DMA((8,)),
-            pltpu.SemaphoreType.DMA((sets,)),
+            pltpu.SemaphoreType.DMA((16,)),
+            pltpu.SemaphoreType.DMA((sets, 2)),
         ],
         compiler_params=pltpu.CompilerParams(vmem_limit_bytes=54 * 1024 * 1024),
         name="pack",

time: 121 us -> 121 us (level)
  no operation moved by 1% of the time
where the time goes in v10:
time: 121 us
  blocking collectives  86.1 us (71%)
  starting transfers between devices  13.3 us (11%)
  Pallas kernels  10 us (8%)
  waiting for transfers between devices  9.28 us (8%)
  other arithmetic  1.23 us (1%)
    all_to_all x2, blocking collectives, summed_over(): lax.all_to_all(partial, AXES, split_axis=0, concat_axis=0, tiled=True, ax...  55.1 us
    all_to_all x1, blocking collectives, shards(): lax.all_to_all(packed, AXES, split_axis=0, concat_axis=0, tiled=True, axi...  31 us
    ppermute x1, starting transfers between devices, shards(): arrived = lax.ppermute(other, 'core', [(0, 1), (1, 0)])  11.3 us
    ppermute x1, waiting for transfers between devices, shards(): held = lax.ppermute(held, AXES, owner_route())  6.64 us
    pallas_call x2, Pallas kernels, blocks(): pl.pallas_call(functools.partial(blocks_kernel, own=own), in_specs=[pl.Bl...  3.52 us
    pallas_call x1, Pallas kernels, pack(): pl.pallas_call(functools.partial(pack_kernel, total_rows=total_rows), in_...  3.42 us
    ppermute x1, waiting for transfers between devices, shards(): arrived = lax.ppermute(other, 'core', [(0, 1), (1, 0)])  2.65 us
  transfers between devices with their start and end apart: 2, of which 2 were waited for; matrix products, arithmetic and copies ran while one was open for 0% of the time, Pallas kernels for 3%

profile of v10, /device:TPU:48, one launch (start us, length us, event | category | flops | bytes accessed | tf_op | source)
XLA Modules:
  0.0 120.6 jit_solution(4992063188051606483)
XLA Ops:
  0.7 3.4 %pack.1 = bf16[8,64,3840]{2,1,0:T(8,128)(2,1)} custom-call(f32[1]{0:T(128)S(6)} %copy.7.freq_hbm, f32[4096]{0:T(1024)} %surface_hbm.1, s32[1024]{0:T(1024)} %picks_hbm.1, bf16[64,24576]{1,0:T(8,128)(2,1)} %bitcast.9), custom_call_target="tpu_custom_call" | custom-call | tf_op jit(solution)/shard_map/pack/pallas_call | solution.py:108
  4.1 31.0 %all_to_all.15 = bf16[8,64,3840]{2,1,0:T(8,128)(2,1)S(1)} all-to-all(bf16[8,64,3840]{2,1,0:T(8,128)(2,1)} %pack.1), channel_id=1, replica_groups={{0,2,64,66,32,34,96,98},{1,7,449,455,57,63,505,511},{5,3,453,451,61,59,..., dimensions={0} | all-to-all | bytes 7864320 | tf_op jit(solution)/shard_map/all_to_all | solution.py:296
  35.1 1.8 %blocks.3 = bf16[4,2,4,312,128]{4,3,2,1,0:T(8,128)(2,1)S(1)} custom-call(bf16[512,3840]{1,0:T(8,128)(2,1)S(1)} %bitcast.5), custom_call_target="tpu_custom_call" | custom-call | flops 1476395008 | bytes 5701632 | tf_op jit(solution)/shard_map/blocks/pallas_call | solution.py:184
  36.8 11.3 %collective-permute-start = (bf16[4,2,4,312,128]{4,3,2,1,0:T(8,128)(2,1)S(1)}, bf16[4,2,4,312,128]{4,3,2,1,0:T(8,128)(2,1)S(1)}, u32[]{:S(2)}, u32[]{:S(2)}) collective-permute-start(bf16[4,2,4,312,128]{4,3,2,1,0:T(8,128)(2,1)S(1)} %blocks.3), channel_id=1, source_target_pairs={{0,1},{1,0},{2,3},{3,2},{4,5},{5,4},{6,7},{7,6},{8,9},{9,8},{10,11... | collective-permute-start | bytes 7667720 | tf_op jit(solution)/shard_map/ppermute | solution.py:299
  48.2 1.8 %blocks.2 = bf16[4,2,4,312,128]{4,3,2,1,0:T(8,128)(2,1)S(1)} custom-call(bf16[512,3840]{1,0:T(8,128)(2,1)S(1)} %bitcast.6), custom_call_target="tpu_custom_call" | custom-call | flops 1476395008 | bytes 5701632 | tf_op jit(solution)/shard_map/blocks/pallas_call | solution.py:184
  50.0 2.6 %collective-permute-done = bf16[4,2,4,312,128]{4,3,2,1,0:T(8,128)(2,1)S(1)} collective-permute-done((bf16[4,2,4,312,128]{4,3,2,1,0:T(8,128)(2,1)S(1)}, bf16[4,2,4,312,128]{4,3,2,1,0:T(8,128)(2,1)S(1)}, u32[]{:S(2)}, u32[]{:S(2)}) %collective-permute-start) | collective-permute-done | bytes 2555936 | tf_op jit(solution)/shard_map/ppermute | solution.py:299
  52.6 0.7 add_convert_fusion
  53.3 41.5 %all_to_all.16 = bf16[8,1248,128]{2,1,0:T(8,128)(2,1)S(1)} all-to-all(bf16[8,1248,128]{2,1,0:T(8,128)(2,1)S(1)} %bitcast.8), channel_id=1, replica_groups={{0,4,128,132,256,260,384,388},{1,5,9,13,17,21,25,29},{2,6,130,134,258,2..., dimensions={0} | all-to-all | bytes 5111808 | tf_op jit(solution)/shard_map/all_to_all | solution.py:286
  94.7 0.0 copy-start
  94.7 0.0 copy-start.1
  94.7 0.5 reduce_sum.24
  95.2 13.6 %all_to_all.17 = bf16[4,312,128]{2,1,0:T(8,128)(2,1)S(1)} all-to-all(bf16[4,312,128]{2,1,0:T(8,128)(2,1)S(1)} %bitcast.10), channel_id=1, replica_groups={{0,8,16,24},{1,129,257,385},{2,10,18,26},{3,131,259,387},{4,12,20,28},{..., dimensions={0} | all-to-all | bytes 638976 | tf_op jit(solution)/shard_map/all_to_all | solution.py:286
  108.9 1.9 %collective-permute-start.1 = (bf16[312,128]{1,0:T(8,128)(2,1)S(1)}, bf16[312,128]{1,0:T(8,128)(2,1)S(1)}, u32[]{:S(2)}, u32[]{:S(2)}) collective-permute-start(bf16[312,128]{1,0:T(8,128)(2,1)S(1)} %reduce_sum.25), channel_id=1, source_target_pairs={{0,0},{1,1},{2,4},{3,5},{4,2},{5,3},{6,6},{7,7},{8,64},{9,65},{10,... | collective-permute-start | bytes 239624 | tf_op jit(solution)/shard_map/ppermute | solution.py:304
  110.8 0.0 copy-done
  110.9 0.0 copy-done.1
  110.9 1.6 %block_index.1.index_ref = s32[6,13]{1,0:T(8,128)S(1)} custom-call(s32[6,13]{1,0:T(8,128)S(1)} %copy-done, s32[6,12]{1,0:T(8,128)S(1)} %copy-done.1), custom_call_target="tpu_custom_call" | custom-call | tf_op jit(solution)/shard_map/block_index/pallas_call | solution.py:210
  112.5 6.6 %collective-permute-done.1 = bf16[312,128]{1,0:T(8,128)(2,1)S(1)} collective-permute-done((bf16[312,128]{1,0:T(8,128)(2,1)S(1)}, bf16[312,128]{1,0:T(8,128)(2,1)S(1)}, u32[]{:S(2)}, u32[]{:S(2)}) %collective-permute-start.1) | collective-permute-done | bytes 79904 | tf_op jit(solution)/shard_map/ppermute | solution.py:304
  119.1 1.4 %slots.1 = bf16[6,13,8,128]{3,2,1,0:T(8,128)(2,1)} custom-call(s32[6,13]{1,0:T(8,128)S(1)} %block_index.1.index_ref, bf16[39,8,128]{2,1,0:T(8,128)(2,1)S(1)} %bitcast.7), custom_call_target="tpu_custom_call" | custom-call | tf_op jit(solution)/shard_map/slots/pallas_call | solution.py:230
  (1 shorter events, 0.0 us)
Async XLA Ops:
  36.8 15.8 %collective-permute-start = (bf16[4,2,4,312,128]{4,3,2,1,0:T(8,128)(2,1)S(1)}, bf16[4,2,4,312,128]{4,3,2,1,0:T(8,128)(2,1)S(1)}, u32[]{:S(2)}, u32[]{:S(2)}) collective-permute-start(bf16[4,2,4,312,128]{4,3,2,1,0:T(8,128)(2,1)S(1)} %blocks.3), channel_id=1, source_target_pairs={{0,1},{1,0},{2,3},{3,2},{4,5},{5,4},{6,7},{7,6},{8,9},{9,8},{10,11... | collective-permute-start | bytes 7667720 | tf_op jit(solution)/shard_map/ppermute | solution.py:299
  94.7 16.1 %copy-start = (s32[6,13]{1,0:T(8,128)S(1)}, s32[6,13]{1,0:T(8,128)}, u32[]{:S(2)}) copy-start(s32[6,13]{1,0:T(8,128)} %neighbours_ref) | copy-start | bytes 940
  94.7 16.1 %copy-start.1 = (s32[6,12]{1,0:T(8,128)S(1)}, s32[6,12]{1,0:T(8,128)}, u32[]{:S(2)}) copy-start(s32[6,12]{1,0:T(8,128)} %constant.6.clone.table_ref) | copy-start | bytes 868
  108.9 10.2 %collective-permute-start.1 = (bf16[312,128]{1,0:T(8,128)(2,1)S(1)}, bf16[312,128]{1,0:T(8,128)(2,1)S(1)}, u32[]{:S(2)}, u32[]{:S(2)}) collective-permute-start(bf16[312,128]{1,0:T(8,128)(2,1)S(1)} %reduce_sum.25), channel_id=1, source_target_pairs={{0,0},{1,1},{2,4},{3,5},{4,2},{5,3},{6,6},{7,7},{8,64},{9,65},{10,... | collective-permute-start | bytes 239624 | tf_op jit(solution)/shard_map/ppermute | solution.py:304
